TPU v7x, 512 devices: a whole 4x4x16 slice. The times are simulated.
512 devices in a mesh: kv: 128 (over x, z, core), pair: 4 (over y).
Axes of the slice: x: 4, y: 4, z: 16, core: 2. Of those that a mesh axis runs over, the one named last changes fastest.
Arguments:
- query: bfloat16 [16, 8192], P(None, ('kv', 'pair')), may hold values from -27 to 27
- key_cache: bfloat16 [16, 16384, 512], P(None, ('kv', 'pair')), may hold values from -9 to 9
- value_cache: bfloat16 [16, 16384, 512], P(None, ('kv', 'pair')), may hold values from -6 to 6
- lengths: int32 [16], replicated, may hold values from 2049 to 16384, as said below
- hidden_in: bfloat16 [16, 4096], P(None, ('kv', 'pair')), may hold values from -40 to 40
- out_proj: bfloat16 [8192, 4096], P(('kv', 'pair')), may hold values from -0.25 to 0.25
- norm_gain: bfloat16 [4096], replicated, may hold values from 0.099609375 to 1.8984375
- expert_ids: int32 [16, 8], replicated, may hold values from 0 to 63, all different within a row; in each aligned block of 16 rows (0 to 15, 16 to 31, ...) at most 4 rows name the same one
- route_weights: float32 [16, 8], replicated, may hold values from 0.1 to 1
- w_gate: bfloat16 [65536, 4096], P(('kv', 'pair')), may hold values from -0.09375 to 0.09375
- w_up: bfloat16 [65536, 4096], P(('kv', 'pair')), may hold values from -0.09375 to 0.09375
- w_down: bfloat16 [65536, 4096], P(('kv', 'pair')), may hold values from -0.75 to 0.75
Outputs:
- context: bfloat16 [16, 8192], P(None, ('kv', 'pair'))
- layer_out: bfloat16 [16, 4096], P(None, ('kv', 'pair'))
Inputs may be any that keep to these rules, and one draw needn't show every extreme that they name: `lengths`: every sequence uses its first positions; some sequence uses all 16384. `expert_ids`: each row names 8 different experts; every expert is named by some row, none by more than 4 rows, and one by exactly 4.
All inputs are finite; a program needn't handle non-finite values.
Results may differ from a plain program's by a relative error of at most 0.01155.
Values may be sent and summed in bfloat16 or wider, within the bound.
No kernel may reach another device: no remote copies, remote signals or barrier semaphores. Data moves between devices by JAX's collectives and lax.ppermute only.
A program may use at most 64 MiB of HBM per device.

v0:
```python
import math

import jax
import jax.numpy as jnp
from jax import lax
from jax.sharding import PartitionSpec as P

H = 64
KVH = 4
HD = 128
FE = 1024
B = 16


floor_score = -1e30


def merged_2(part, axis, combine):
    gathered = jax.tree.map(lambda a: lax.all_gather(a, axis), part)

    def take(source):
        return jax.tree.map(lambda a: lax.dynamic_index_in_dim(a, source, 0, False), gathered)

    return lax.fori_loop(
        1, lax.axis_size(axis), lambda source, state: combine(state, take(source)), take(0)
    )


def slot_tables(expert_ids, share, count, slot_count):
    experts = jnp.arange(count, dtype=jnp.int32)
    match = expert_ids[None, :, :] == experts[:, None, None]
    hits = jnp.sum(match.astype(jnp.int32), axis=2)
    weight = jnp.sum(jnp.where(match, share[None, :, :], 0.0), axis=2)
    order = jnp.cumsum(hits, axis=1) - hits
    slots = jnp.arange(slot_count, dtype=jnp.int32)
    table = ((hits[:, None, :] == 1) & (order[:, None, :] == slots[None, :, None])).astype(
        jnp.float32
    )
    coefficient = jnp.sum(table * weight[:, None, :], axis=2)
    return (table, coefficient)


def join(first, second):
    first_mixed, first_top, first_total = first
    second_mixed, second_top, second_total = second
    highest = jnp.maximum(first_top, second_top)
    first_scale = jnp.exp(first_top - highest)
    second_scale = jnp.exp(second_top - highest)
    mixed = first_mixed * first_scale[..., None] + second_mixed * second_scale[..., None]
    return (mixed, highest, first_total * first_scale + second_total * second_scale)


def attend(queries, keys, values, first_place, lengths):
    batch = keys.shape[0]
    count = keys.shape[1]
    groups = queries.shape[1]
    per_group = queries.shape[2]
    head_size = queries.shape[3]
    keys = keys.reshape(batch, count, groups, head_size)
    values = values.reshape(batch, count, groups, head_size)
    scores = jnp.einsum(
        "bgqd,btgd->bgqt", queries, keys, preferred_element_type=jnp.float32
    ) / math.sqrt(head_size)
    places = first_place + jnp.arange(count, dtype=jnp.int32)
    valid = (places[None, :] < lengths[:, None])[:, None, None, :]
    scores = jnp.where(valid, scores, floor_score)
    highest = jnp.max(scores, axis=-1)
    weights = jnp.where(valid, jnp.exp(scores - highest[..., None]), 0.0)
    total = jnp.sum(weights, axis=-1)
    mixed = jnp.einsum(
        "bgqt,btgd->bgqd", weights, values.astype(jnp.float32), precision=lax.Precision.HIGHEST
    )
    heads = groups * per_group
    return (
        mixed.reshape(batch, heads, head_size),
        highest.reshape(batch, heads),
        total.reshape(batch, heads),
    )


def to_units(mixed, highest, total, kv_count, pair_count, unit_size):
    batch = mixed.shape[0]
    heads = mixed.shape[1]
    head_size = mixed.shape[2]
    per_head = head_size // unit_size
    block_units = heads * per_head // (kv_count * pair_count)
    mixed = mixed.reshape(batch, kv_count, pair_count, block_units, unit_size)
    highest = jnp.repeat(highest, per_head, axis=1).reshape(
        batch, kv_count, pair_count, block_units
    )
    total = jnp.repeat(total, per_head, axis=1).reshape(batch, kv_count, pair_count, block_units)
    return (mixed, highest, total)


def fold_sources(mixed, highest, total, source_axis):
    best = jnp.max(highest, axis=source_axis, keepdims=True)
    scale = jnp.exp(highest - best)
    merged_mixed = jnp.sum(mixed * scale[..., None], axis=source_axis)
    merged_total = jnp.sum(total * scale, axis=source_axis)
    return (merged_mixed, jnp.squeeze(best, axis=source_axis), merged_total)


def shards(
    query,
    key_cache,
    value_cache,
    lengths,
    hidden_in,
    out_proj,
    norm_gain,
    expert_ids,
    route_weights,
    w_gate,
    w_up,
    w_down,
):
    kv_count = lax.axis_size("kv")
    pair_count = lax.axis_size("pair")
    kv_index = lax.axis_index("kv")
    pair_index = lax.axis_index("pair")
    block_index = kv_index * pair_count + pair_index
    feature_share = query.shape[1]
    column_share = hidden_in.shape[1]
    local_span = key_cache.shape[1]
    unit_size = min(feature_share, HD)
    gathered_query, gathered_hidden = (
        lax.all_gather(query, ("kv", "pair"), axis=1, tiled=True),
        lax.all_gather(hidden_in, ("kv", "pair"), axis=1, tiled=True),
    )
    queries = gathered_query.reshape(B, KVH, H // KVH, HD)

    def own_pair(piece):
        return lax.dynamic_index_in_dim(piece, pair_index, 2, keepdims=False)

    part_mixed, part_top, part_total = attend(
        queries, key_cache, value_cache, block_index * local_span, lengths
    )
    merged = merged_2((part_mixed, part_top, part_total), "pair", join)
    unit_mixed, unit_top, unit_total = to_units(
        merged[0], merged[1], merged[2], kv_count, pair_count, unit_size
    )
    send_mixed, send_top, send_total = (
        own_pair(unit_mixed),
        own_pair(unit_top),
        own_pair(unit_total),
    )
    arrived = (
        lax.all_to_all(send_mixed, "kv", split_axis=1, concat_axis=1, tiled=True),
        lax.all_to_all(send_top, "kv", split_axis=1, concat_axis=1, tiled=True),
        lax.all_to_all(send_total, "kv", split_axis=1, concat_axis=1, tiled=True),
    )
    final_mixed, final_top, final_total = fold_sources(arrived[0], arrived[1], arrived[2], 1)
    context = (final_mixed / final_total[..., None]).reshape(B, feature_share).astype(jnp.bfloat16)
    term = jnp.dot(context, out_proj, preferred_element_type=jnp.float32)
    projected = lax.psum(term, ("kv", "pair"))
    mid = (gathered_hidden.astype(jnp.float32) + projected).astype(jnp.bfloat16)
    mid_part = lax.dynamic_slice_in_dim(mid, block_index * column_share, column_share, 1)
    mid_float = mid.astype(jnp.float32)
    scale = lax.rsqrt(jnp.mean(mid_float * mid_float, axis=-1, keepdims=True) + 1e-06)
    normed = (mid_float * scale * norm_gain.astype(jnp.float32)[None, :]).astype(jnp.bfloat16)
    share = route_weights / jnp.sum(route_weights, axis=-1, keepdims=True)
    choose_count = expert_ids.shape[1]
    group_size = FE // w_gate.shape[0]
    expert_count = kv_count * pair_count // group_size
    slot_count = min(B, 2 * ((B * choose_count + expert_count - 1) // expert_count))
    table, coefficient = slot_tables(expert_ids, share, expert_count, slot_count)
    expert_index = block_index // group_size
    own_table = lax.dynamic_index_in_dim(table, expert_index, 0, keepdims=False)
    own_coefficient = lax.dynamic_index_in_dim(coefficient, expert_index, 0, keepdims=False)
    picked = jnp.dot(
        own_table.astype(jnp.bfloat16), normed, preferred_element_type=jnp.float32
    ).astype(jnp.bfloat16)
    gate = jnp.einsum("cd,fd->cf", picked, w_gate, preferred_element_type=jnp.float32)
    upward = jnp.einsum("cd,fd->cf", picked, w_up, preferred_element_type=jnp.float32)
    hidden_units = (jax.nn.silu(gate) * upward).astype(jnp.bfloat16)
    weighted = (
        jnp.dot(hidden_units, w_down, preferred_element_type=jnp.float32) * own_coefficient[:, None]
    )
    spread_back = jnp.einsum("cb,cd->bd", own_table, weighted, precision=lax.Precision.HIGHEST)
    mixture_part = lax.psum_scatter(spread_back, ("kv", "pair"), scatter_dimension=1, tiled=True)
    layer_out = (mid_part.astype(jnp.float32) + mixture_part).astype(jnp.bfloat16)
    return (context, layer_out)


def solution(mesh):
    placed = (
        P(None, ("kv", "pair")),
        P(None, ("kv", "pair"), None),
        P(None, ("kv", "pair"), None),
        P(),
        P(None, ("kv", "pair")),
        P(("kv", "pair"), None),
        P(),
        P(),
        P(),
        P(("kv", "pair"), None),
        P(("kv", "pair"), None),
        P(("kv", "pair"), None),
    )
    return jax.shard_map(
        shards,
        mesh=mesh,
        in_specs=placed,
        out_specs=(P(None, ("kv", "pair")), P(None, ("kv", "pair"))),
        check_vma=False,
    )
```

profile of v0, /device:TPU:1, one launch (start us, length us, event | category | flops | bytes accessed | tf_op | source)
XLA Modules:
  0.0 1251.6 jit_solution(17527940853227639309)
XLA Ops:
  7.2 0.8 copy.59
  8.1 205.0 %all_gather.15 = bf16[16,8192]{0,1:T(8,128)(2,1)S(1)} all-gather(bf16[16,16]{0,1:T(8,128)(2,1)S(1)} %copy.59), channel_id=1, replica_groups=mesh['kv'=128,'pair'=4] {'kv','pair'}, dimensions={1}, use_global_device_ids=true | all-gather | bytes 262656 | tf_op jit(solution)/shard_map/all_gather | solution.py:127
  213.1 1.0 copy.79
  214.2 1.5 fusion.35
  215.7 2.5 fusion.5
  218.3 0.4 fusion.10
  218.9 9.0 all_gather.18
  227.9 9.4 all_gather.17
  237.5 13.9 %all-gather.2.cloned.1.call-done = f32[4,16,64,128]{3,2,1,0:T(8,128)} async-done(((f32[1,16,64,128]{3,2,1,0:T(8,128)}), f32[4,16,64,128]{3,2,1,0:T(8,128)}) %all-gather.2.cloned.1.call-update) | async-done | bytes 2097168 | tf_op jit(solution)/shard_map/all_gather | solution.py:19
  251.4 1.1 slice_bitcast_fusion
  252.5 4.8 while.19
  252.6 1.5 fusion.52
  254.2 1.5 fusion.52
  255.8 1.5 fusion.52
  257.4 0.7 broadcast_in_dim.63
  258.1 16.5 %all-to-all-start.1 = ((f32[16,128,1]{0,2,1:T(1,128)}), f32[16,128,1]{0,2,1:T(1,128)S(1)}, u32[]{:S(2)}, u32[]{:S(2)}) async-start(f32[16,128,1]{0,2,1:T(1,128)} %bitcast.10), calls=%async_computation.1 | async-start | bytes 131072 | tf_op jit(solution)/shard_map/all_to_all | solution.py:149
  274.6 0.2 reduce_window_sum.11
  274.8 0.1 copy.71
  275.0 4.1 reshape.109
  279.2 10.3 all-to-all-done.1
  289.5 0.7 broadcast_in_dim.64
  290.2 6.5 all-to-all-start.2
  296.7 3.3 constant_dynamic-slice_fusion.2
  300.0 0.6 copy.97
  300.7 1.0 reshape.112
  301.7 10.1 all-to-all-done.2
  311.8 6.6 all-to-all-start
  318.5 0.1 select_reduce_fusion.1
  318.7 0.2 select_reduce_fusion
  318.8 0.2 reduce_max.19
  319.0 0.2 multiply_reduce_fusion.1
  319.1 16.8 %all-to-all-done = f32[128,1,256]{2,1,0:T(1,128)S(1)} async-done(((f32[128,1,256]{2,1,0:T(1,128)}), f32[128,1,256]{2,1,0:T(1,128)S(1)}, u32[]{:S(2)}, u32[]{:S(2)}) %all-to-all-start) | async-done | bytes 131104 | tf_op jit(solution)/shard_map/all_to_all | solution.py:148
  335.9 0.5 broadcast.78
  336.5 1.0 reduce.3
  337.4 0.3 reshape.113
  337.8 0.3 multiply_reduce_fusion
  338.2 0.9 fusion.36
  339.1 230.0 %all_gather.19 = bf16[16,4096]{0,1:T(8,128)(2,1)S(1)} all-gather(bf16[16,8]{0,1:T(8,128)(2,1)S(1)} %copy-done.7), channel_id=1, replica_groups=mesh['kv'=128,'pair'=4] {'kv','pair'}, dimensions={1}, use_global_device_ids=true | all-gather | bytes 131328 | tf_op jit(solution)/shard_map/all_gather | solution.py:128
  569.2 0.3 copy.69
  569.5 215.0 %all-reduce.4.cloned.1.call-done = f32[16,4096]{1,0:T(8,128)} async-done(((f32[16,4096]{1,0:T(8,128)}), f32[16,4096]{1,0:T(8,128)}) %all-reduce.4.cloned.1.call-update) | async-done | bytes 262160 | tf_op jit(solution)/shard_map/psum | solution.py:155
  784.5 1.1 fusion.11
  785.6 0.2 convolution_convert_fusion
  785.9 0.4 fusion.37
  786.2 2.1 convolution_multiply_fusion
  788.4 1.1 fusion.25
  789.5 454.2 %all-reduce.6.cloned.1.call-done = f32[16,4096]{1,0:T(8,128)} async-done(((f32[16,4096]{1,0:T(8,128)}), f32[16,4096]{1,0:T(8,128)}) %all-reduce.6.cloned.1.call-update) | async-done | bytes 262160
  1243.7 0.8 fusion.21
  1244.4 0.7 copy.77
  (48 shorter events, 1.2 us)
Async XLA Ops:
  7.2 779.1 %copy-start = (bf16[128,4096]{1,0:T(8,128)(2,1)S(1)}, bf16[128,4096]{1,0:T(8,128)(2,1)}, u32[]{:S(2)}) copy-start(bf16[128,4096]{1,0:T(8,128)(2,1)} %param.25) | copy-start | bytes 3145732
  7.2 244.3 %all-gather.2.cloned.1.call-start = ((), (), s32[]{:S(2)}) async-start(), calls=%async_computation.3 | async-start | bytes 2621440 | tf_op jit(solution)/shard_map/all_gather | solution.py:19
  8.1 206.0 %copy-start.8 = (s32[16]{0:T(128)S(1)}, s32[16]{0:T(128)}, u32[]{:S(2)}) copy-start(s32[16]{0:T(128)} %param.17) | copy-start | bytes 196
  214.1 4.7 copy-start.6
  214.1 4.8 copy-start.4
  258.1 31.5 %all-to-all-start.1 = ((f32[16,128,1]{0,2,1:T(1,128)}), f32[16,128,1]{0,2,1:T(1,128)S(1)}, u32[]{:S(2)}, u32[]{:S(2)}) async-start(f32[16,128,1]{0,2,1:T(1,128)} %bitcast.10), calls=%async_computation.1 | async-start | bytes 131072 | tf_op jit(solution)/shard_map/all_to_all | solution.py:149
  290.2 21.6 %all-to-all-start.2 = ((f32[16,128,1]{0,2,1:T(1,128)}), f32[16,128,1]{0,2,1:T(1,128)S(1)}, u32[]{:S(2)}, u32[]{:S(2)}) async-start(f32[16,128,1]{0,2,1:T(1,128)} %bitcast.13), calls=%async_computation.2 | async-start | bytes 131072 | tf_op jit(solution)/shard_map/all_to_all | solution.py:150
  300.6 37.5 %copy-start.2 = (bf16[16,4096]{1,0:T(8,128)(2,1)S(1)}, bf16[16,4096]{1,0:T(8,128)(2,1)}, u32[]{:S(2)}) copy-start(bf16[16,4096]{1,0:T(8,128)(2,1)} %param.19) | copy-start | bytes 393220
  301.7 37.4 %copy-start.7 = (bf16[16,8]{0,1:T(8,128)(2,1)S(1)}, bf16[16,8]{0,1:T(8,128)(2,1)}, u32[]{:S(2)}) copy-start(bf16[16,8]{0,1:T(8,128)(2,1)} %param.18) | copy-start | bytes 772
  311.8 24.1 %all-to-all-start = ((f32[128,1,256]{2,1,0:T(1,128)}), f32[128,1,256]{2,1,0:T(1,128)S(1)}, u32[]{:S(2)}, u32[]{:S(2)}) async-start(f32[128,1,256]{2,1,0:T(1,128)} %reshape.112), calls=%async_computation | async-start | bytes 262144 | tf_op jit(solution)/shard_map/all_to_all | solution.py:148
  318.4 466.1 %all-reduce.4.cloned.1.call-start = ((), (), s32[]{:S(2)}) async-start(), calls=%async_computation.4 | async-start | bytes 524288 | tf_op jit(solution)/shard_map/psum | solution.py:155
  337.7 231.8 %copy-start.5 = (bf16[4096]{0:T(1024)(128)(2,1)S(1)}, bf16[4096]{0:T(1024)(128)(2,1)}, u32[]{:S(2)}) copy-start(bf16[4096]{0:T(1024)(128)(2,1)} %param.20) | copy-start | bytes 24580
  338.1 447.8 %copy-start.1 = (bf16[128,4096]{1,0:T(8,128)(2,1)S(1)}, bf16[128,4096]{1,0:T(8,128)(2,1)}, u32[]{:S(2)}) copy-start(bf16[128,4096]{1,0:T(8,128)(2,1)} %param.23) | copy-start | bytes 3145732
  338.2 448.0 %copy-start.3 = (bf16[16,16]{1,0:T(8,128)(2,1)}, bf16[16,16]{1,0:T(8,128)(2,1)S(1)}, u32[]{:S(2)}) copy-start(bf16[16,16]{1,0:T(8,128)(2,1)S(1)} %divide_convert_fusion) | copy-start | bytes 1540
  339.1 904.6 %all-reduce.6.cloned.1.call-start = ((), (), s32[]{:S(2)}) async-start(), calls=%async_computation.5 | async-start | bytes 524288
Sparse Core Ops, SparseCore 0:
  218.4 33.0 all-gather.1
  339.2 445.2 all-reduce.3
  790.8 452.7 all-reduce.5
where the time goes:
time: 1250 us
  waiting for transfers between devices  720 us (58%)
  blocking collectives  454 us (36%)
  starting transfers between devices  29.7 us (2%)
  local copies, waits for them, and re-layouts  15.9 us (1%)
  between operations  14 us (1%)
    unnamed x4, waiting for transfers between devices  454 us
    all_gather x1, blocking collectives, shards(): lax.all_gather(hidden_in, ('kv', 'pair'), axis=1, tiled=True)  230 us
    psum x1, waiting for transfers between devices, shards(): projected = lax.psum(term, ('kv', 'pair'))  215 us
    all_gather x1, blocking collectives, shards(): lax.all_gather(query, ('kv', 'pair'), axis=1, tiled=True)  205 us
  transfers between devices with their start and end apart: 6, of which 6 were waited for; matrix products, arithmetic and copies ran while one was open for 1% of the time, Pallas kernels for 0%

commit v1 on v0

v1 whole, which is shorter than its diff:
```python
import math

import jax
import jax.numpy as jnp
import numpy as np
from jax import lax
from jax.experimental import pallas as pl
from jax.experimental.pallas import tpu as pltpu
from jax.sharding import Mesh
from jax.sharding import PartitionSpec as P

HD = 128
X, Z, CY = 4, 16, 8
PLANE = X * CY
B = 16
D = 4096
SPAN = 32
FLOOR = -1e30
BF = jnp.bfloat16
F32 = jnp.float32
PLANE_AXES = ("x", "c", "y")
ALL_AXES = ("x", "z", "c", "y")


def iota(shape, dimension):
    return lax.broadcasted_iota(jnp.int32, shape, dimension)


def dot(a, b, dims, precision=None):
    return lax.dot_general(
        a, b, (dims, ((), ())), preferred_element_type=F32, precision=precision
    )


def eye(n, dtype=BF):
    return (iota((n, n), 0) == iota((n, n), 1)).astype(dtype)


def spread_query(arrived, out):
    rows = arrived[...].astype(F32).reshape(Z * 8, 48).astype(BF)
    turned = dot(rows, eye(Z * 8), ((0,), (0,))).astype(BF)
    for k in range(PLANE):
        out[k] = turned


def attend(place, lengths, gathered, keys, values, out, hidden_block):
    device = place[0]
    x, cy = place[1], place[3]
    lane_j = iota((SPAN, 128), 1) % 8
    position = device * SPAN + iota((SPAN, 128), 0)
    zeros = jnp.zeros((10, 128), F32)
    valids = []
    for i in range(2):
        valids.append(
            jnp.concatenate(
                [
                    ((lane_j == j) & (position < lengths[i * 8 + j])).astype(F32)
                    for j in range(8)
                ],
                axis=0,
            )
        )
    for g in range(X):
        stats = [[], [], []]
        for i in range(2):
            query = gathered[g * CY : (g + 1) * CY, i * 16 : (i + 1) * 16, :].reshape(HD, 128)
            k = keys[i * 8 : (i + 1) * 8, :, g * HD : (g + 1) * HD].reshape(8 * SPAN, HD)
            v = values[i * 8 : (i + 1) * 8, :, g * HD : (g + 1) * HD].reshape(8 * SPAN, HD)
            scores = dot(k, query, ((1,), (0,))) * (1.0 / math.sqrt(HD))
            valid = valids[i] > 0.5
            scores = jnp.where(valid, scores, FLOOR)
            top = jnp.max(scores, axis=0, keepdims=True).astype(BF).astype(F32)
            weights = jnp.where(valid, jnp.exp(scores - top), 0.0).astype(BF)
            total = jnp.sum(weights.astype(F32), axis=0, keepdims=True)
            mixed = dot(v, weights, ((0,), (0,))).astype(BF)
            for c in range(CY):
                out[g * CY + c, i * 16 : (i + 1) * 16, :] = mixed[c * 16 : (c + 1) * 16]
            high = total.astype(BF).astype(F32)
            stats[0].append(top)
            stats[1].append(high)
            stats[2].append(total - high)
        block = jnp.concatenate(stats[0] + stats[1] + stats[2] + [zeros], axis=0).astype(BF)
        for c in range(CY):
            out[g * CY + c, 32:48, :] = block
    own = gathered[pl.ds(x * CY, CY), 32:48, :]
    row, lane = iota((128, 128), 0), iota((128, 128), 1)
    pick = (row % 8 == lane % 8) & (row // 8 == 2 * cy + lane // 64)
    total = jnp.zeros((B, 128), F32)
    for c in range(CY):
        select = (pick & (lane // 8 % 8 == c)).astype(BF)
        total += dot(own[c], select, ((1,), (0,)))
    hidden_block[...] = total


def merge_plane(arrived, out):
    parts = []
    tops, highs, lows = [], [], []
    for i in range(2):
        top = arrived[:, 32 + i, :].astype(F32)
        total = arrived[:, 34 + i, :].astype(F32) + arrived[:, 36 + i, :].astype(F32)
        best = jnp.max(top, axis=0, keepdims=True)
        scale = jnp.exp(top - best)
        mass = jnp.sum(total * scale, axis=0, keepdims=True)
        mixed = arrived[:, i * 16 : (i + 1) * 16, :].astype(F32)
        parts.append(jnp.sum(mixed * scale[:, None, :], axis=0))
        high = mass.astype(BF).astype(F32)
        tops.append(best)
        highs.append(high)
        lows.append(mass - high)
    full = jnp.concatenate(
        parts + tops + highs + lows + [jnp.zeros((10, 128), F32)], axis=0
    ).astype(BF)
    turned = dot(eye(128), full, ((1,), (1,)))
    out[...] = turned.reshape(Z, 8, 48).astype(BF)


def finish_context(arrived, out_proj, context, out):
    rows = arrived[...].astype(F32).reshape(Z * 8, 48).astype(BF)
    row, lane = iota((48, 32), 0), iota((48, 32), 1)
    mixed = dot(rows, (row == lane).astype(BF), ((1,), (0,))).reshape(Z, 8, 32)
    top = dot(rows, (row == 32 + lane // 16).astype(BF), ((1,), (0,))).reshape(Z, 8, 32)
    both = (row == 34 + lane // 16) | (row == 36 + lane // 16)
    total = dot(rows, both.astype(BF), ((1,), (0,))).reshape(Z, 8, 32)
    scale = jnp.exp(top - jnp.max(top, axis=0, keepdims=True))
    done = jnp.sum(mixed * scale, axis=0) / jnp.sum(total * scale, axis=0)
    twice = jnp.concatenate([done, done], axis=0)
    twice = jnp.where(iota((16, 32), 0) // 8 == iota((16, 32), 1) // 16, twice, 0.0).astype(BF)
    fold = (iota((32, 16), 0) % 16 == iota((32, 16), 1)).astype(BF)
    final = dot(twice, fold, ((1,), (0,))).astype(BF)
    context[...] = final
    term = dot(final, out_proj[...], ((1,), (0,))).astype(BF)
    for k in range(PLANE):
        out[k] = term[:, k * 128 : (k + 1) * 128]


def sum_plane(arrived, out):
    total = jnp.sum(arrived[...].astype(F32), axis=0).astype(BF)
    for z in range(Z):
        out[z] = total


def make_mid(arrived, hidden_block, out):
    mid = (jnp.sum(arrived[...].astype(F32), axis=0) + hidden_block[...]).astype(BF)
    for k in range(PLANE):
        out[k] = mid


def experts(place, mid_blocks, gain, expert_ids, route_weights, w_gate, w_up, w_down, order, out):
    expert = place[4]
    ids = dot(expert_ids[...].astype(F32), eye(B, F32), ((0,), (0,)))
    exact = lax.Precision.HIGHEST
    routes = dot(route_weights[...], eye(B, F32), ((0,), (0,)), exact)
    match = ids == expert.astype(F32)
    hits = jnp.sum(match.astype(F32), axis=0, keepdims=True)
    share = routes / jnp.sum(routes, axis=0, keepdims=True)
    weight = jnp.sum(jnp.where(match, share, 0.0), axis=0, keepdims=True)
    before = (iota((B, B), 0) < iota((B, B), 1)).astype(F32)
    rank = dot(jnp.broadcast_to(hits, (8, B)), before, ((1,), (0,)))
    table = (hits > 0.5) & (jnp.abs(rank - iota((8, B), 0).astype(F32)) < 0.5)
    coefficient = jnp.sum(jnp.where(table, weight, 0.0), axis=1, keepdims=True)
    table = table.astype(BF)
    mid = jnp.concatenate([mid_blocks[k] for k in range(PLANE)], axis=1)
    rows = dot(table, mid, ((1,), (0,)))
    scale = lax.rsqrt(jnp.sum(rows * rows, axis=1, keepdims=True) * (1.0 / D) + 1e-06)
    picked = (rows * scale * gain[...].astype(F32)).astype(BF)
    gate = dot(picked, w_gate[...], ((1,), (1,)))
    upward = dot(picked, w_up[...], ((1,), (1,)))
    hidden_units = (gate / (1.0 + jnp.exp(-gate)) * upward).astype(BF)
    weighted = (dot(hidden_units, w_down[...], ((1,), (0,))) * coefficient).astype(BF)
    back = dot(table, weighted, ((0,), (0,))).astype(BF)
    stacked = jnp.concatenate([back[:, x * 1024 : (x + 1) * 1024] for x in range(X)], axis=0)
    sorted_back = dot(stacked, order[...], ((1,), (0,))).astype(BF)
    for x in range(X):
        for c in range(CY):
            out[x * CY + c] = sorted_back[x * B : (x + 1) * B, c * 128 : (c + 1) * 128]


def sum_experts(arrived, out):
    total = jnp.sum(arrived[...].astype(F32), axis=0).astype(BF)
    turned = dot(eye(128), total, ((1,), (1,)))
    out[...] = turned.reshape(Z, 8, B).astype(BF)


def finish_layer(place, arrived, mid_blocks, out):
    x, z, cy = place[1], place[2], place[3]
    total = jnp.sum(arrived[...].astype(F32), axis=0)
    mixture = dot(total, eye(8, F32), ((0,), (0,)), lax.Precision.HIGHEST)
    tile = mid_blocks[x * CY + z // 2]
    select = iota((128, 8), 0) == z % 2 * 64 + cy * 8 + iota((128, 8), 1)
    mid = dot(tile, select.astype(BF), ((1,), (0,)))
    out[...] = (mid + mixture).astype(BF)


def call(body, outs, scalars, *arrays):
    smem = pl.BlockSpec(memory_space=pltpu.SMEM)
    vmem = pl.BlockSpec(memory_space=pltpu.VMEM)
    single = not isinstance(outs, list)
    results = pl.pallas_call(
        body,
        out_shape=outs,
        in_specs=[smem] * len(scalars) + [vmem] * len(arrays),
        out_specs=vmem if single else [vmem] * len(outs),
        compiler_params=pltpu.CompilerParams(vmem_limit_bytes=24 * 1024 * 1024),
    )(*scalars, *arrays)
    return results


def swap(blocks, axes):
    return lax.all_to_all(blocks, axes, 0, 0, tiled=True)


def block_order():
    columns = np.arange(1024).reshape(Z, CY, 8).transpose(1, 0, 2).reshape(-1)
    order = np.zeros((1024, 1024), np.float32)
    order[columns, np.arange(1024)] = 1.0
    return order.astype(jnp.bfloat16)


def shards(
    query,
    key_cache,
    value_cache,
    lengths,
    hidden_in,
    out_proj,
    norm_gain,
    expert_ids,
    route_weights,
    w_gate,
    w_up,
    w_down,
):
    x, z = lax.axis_index("x"), lax.axis_index("z")
    cy = lax.axis_index("c") * 4 + lax.axis_index("y")
    expert = x * Z + z
    place = jnp.stack([expert * CY + cy, x, z, cy, expert]).astype(jnp.int32)

    def shape(*dims, dtype=BF):
        return jax.ShapeDtypeStruct(dims, dtype)

    own = jnp.concatenate([query[:8], query[8:], hidden_in.T], axis=1)
    along_z = swap(jnp.broadcast_to(own[None], (Z, 8, 48)), "z")
    gathered = swap(call(spread_query, shape(PLANE, 48, 128), (), along_z), PLANE_AXES)
    partial, hidden_block = call(
        attend,
        [shape(PLANE, 48, 128), shape(B, 128, dtype=F32)],
        (place, lengths),
        gathered,
        key_cache,
        value_cache,
    )
    merged = call(merge_plane, shape(Z, 8, 48), (), swap(partial, PLANE_AXES))
    context, term = call(
        finish_context,
        [shape(B, 16), shape(PLANE, B, 128)],
        (),
        swap(merged, "z"),
        out_proj,
    )
    projected = call(sum_plane, shape(Z, B, 128), (), swap(term, PLANE_AXES))
    mid = call(make_mid, shape(PLANE, B, 128), (), swap(projected, "z"), hidden_block)
    mid_blocks = swap(mid, PLANE_AXES)
    mixture = call(
        experts,
        shape(PLANE, B, 128),
        (place,),
        mid_blocks,
        norm_gain.reshape(1, D),
        expert_ids,
        route_weights,
        w_gate,
        w_up,
        w_down,
        jnp.asarray(block_order()),
    )
    summed = call(sum_experts, shape(Z, 8, B), (), swap(mixture, PLANE_AXES))
    layer_out = call(finish_layer, shape(B, 8), (place,), swap(summed, "z"), mid_blocks)
    return context, layer_out


def solution(mesh):
    fine = Mesh(np.asarray(mesh.devices).reshape(X, Z, 2, 4), ALL_AXES)
    columns, rows = P(None, ALL_AXES), P(ALL_AXES, None)
    cache = P(None, ALL_AXES, None)
    placed = (
        columns,
        cache,
        cache,
        P(),
        columns,
        rows,
        P(),
        P(),
        P(),
        rows,
        rows,
        rows,
    )
    return jax.shard_map(
        shards,
        mesh=fine,
        in_specs=placed,
        out_specs=(columns, columns),
        check_vma=False,
    )
```

time: 1250 us -> 158 us (0.13)
  waiting for transfers between devices: 720 us -> 16 us
  blocking collectives: 454 us -> 107 us
  starting transfers between devices: 29.7 us -> 14.8 us
  between operations: 14 us -> 0.73 us
    unnamed x4 -> x0, waiting for transfers between devices: 454 us -> none
    all_gather x4 -> x0, blocking collectives: 454 us -> none  [the longest x1 230 us: shards(): lax.all_gather(hidden_in, ('kv', 'pair'), axis=1, tiled=True)]
    psum x1 -> x0, waiting for transfers between devices: 215 us -> none  [shards(): projected = lax.psum(term, ('kv', 'pair'))]
    all_to_all x0 -> x7, blocking collectives: none -> 107 us  [swap(): return lax.all_to_all(blocks, axes, 0, 0, tiled=True)]
    all_to_all x3 -> x2, waiting for transfers between devices: 37.2 us -> 16 us  [swap(): return lax.all_to_all(blocks, axes, 0, 0, tiled=True)]
    all_to_all x3 -> x2, starting transfers between devices: 29.6 us -> 14.8 us  [swap(): return lax.all_to_all(blocks, axes, 0, 0, tiled=True)]
    all_gather x1 -> x0, waiting for transfers between devices: 13.9 us -> none  [merged_2(): gathered = jax.tree.map(lambda a: lax.all_gather(a, axis), part)]
  transfers between devices with their start and end apart: 6 -> 2, of which waited for: 6 -> 2; matrix products, arithmetic and copies ran while one was open for 1% -> 1% of each run, Pallas kernels for 0% -> 0%
where the time goes in v1:
time: 158 us; the launch traced here: 157 us
  blocking collectives  107 us (68%)
  waiting for transfers between devices  16 us (10%)
  starting transfers between devices  14.8 us (9%)
  local copies, waits for them, and re-layouts  9.54 us (6%)
  Pallas kernels  7.71 us (5%)
    all_to_all x7, blocking collectives, swap(): return lax.all_to_all(blocks, axes, 0, 0, tiled=True)  107 us
    all_to_all x2, waiting for transfers between devices, swap(): return lax.all_to_all(blocks, axes, 0, 0, tiled=True)  16 us
    all_to_all x2, starting transfers between devices, swap(): return lax.all_to_all(blocks, axes, 0, 0, tiled=True)  14.8 us
    unnamed x25, local copies, waits for them, and re-layouts  8.04 us
    pallas_call x9, Pallas kernels, call(): pl.pallas_call(body, out_shape=outs, in_specs=[smem] * len(scalars) + [vm...  7.71 us
  transfers between devices with their start and end apart: 2, of which 2 were waited for; matrix products, arithmetic and copies ran while one was open for 1% of the time, Pallas kernels for 0%

profile of v1, /device:TPU:1, one launch (start us, length us, event | category | flops | bytes accessed | tf_op | source)
XLA Modules:
  0.0 156.7 jit_solution(1038759037128851393)
XLA Ops:
  0.6 0.7 fusion
  1.3 0.8 pad_maximum_fusion
  2.1 0.1 reshape.9
  2.2 26.9 %all_to_all.45 = bf16[16,2,192]{2,1,0:T(2,128)(2,1)S(1)} all-to-all(bf16[16,2,192]{2,1,0:T(2,128)(2,1)S(1)} %reshape.9), channel_id=1, replica_groups=mesh['x'=4,'z'=16,'c'=2,'y'=4] {'z'}, dimensions={0} | all-to-all | bytes 24576 | tf_op jit(solution)/shard_map/all_to_all | solution.py:209
  29.1 0.1 reshape.10.arrived
  29.2 0.9 shard_map.140
  30.2 0.0 copy-start.8
  30.2 9.3 %all-to-all-start.1 = ((bf16[32,48,128]{2,1,0:T(8,128)(2,1)}), bf16[32,48,128]{2,1,0:T(8,128)(2,1)S(1)}, u32[]{:S(2)}, u32[]{:S(2)}) async-start(bf16[32,48,128]{2,1,0:T(8,128)(2,1)} %shard_map.140), calls=%async_computation.1 | async-start | bytes 786432 | tf_op jit(solution)/shard_map/all_to_all | solution.py:209
  39.5 0.0 copy-start
  39.5 0.0 copy-start.1
  39.5 0.1 stack.23.place
  39.6 9.9 %all-to-all-done.1.gathered = bf16[32,48,128]{2,1,0:T(8,128)(2,1)S(1)} async-done(((bf16[32,48,128]{2,1,0:T(8,128)(2,1)}), bf16[32,48,128]{2,1,0:T(8,128)(2,1)S(1)}, u32[]{:S(2)}, u32[]{:S(2)}) %all-to-all-start.1) | async-done | bytes 393248 | tf_op jit(solution)/shard_map/all_to_all | solution.py:209
  49.5 0.0 copy-start.4
  49.5 1.0 copy-done.4
  50.6 0.0 copy-start.5
  50.6 1.0 copy-done.5
  51.6 0.0 copy-start.7
  51.6 0.7 copy-done.7
  52.3 1.5 shard_map.141
  53.7 14.0 %all_to_all.46.arrived = bf16[32,48,128]{2,1,0:T(8,128)(2,1)S(1)} all-to-all(bf16[32,48,128]{2,1,0:T(8,128)(2,1)S(1)} %get-tuple-element.6), channel_id=1, replica_groups=mesh['x'=4,'z'=16,'c'=2,'y'=4] {'x','c','y'}, dimensions={0} | all-to-all | bytes 786432 | tf_op jit(solution)/shard_map/all_to_all | solution.py:209
  67.8 0.3 shard_map.142
  68.1 0.1 reshape.11
  68.2 13.8 %all_to_all.47 = bf16[16,2,192]{2,1,0:T(2,128)(2,1)S(1)} all-to-all(bf16[16,2,192]{2,1,0:T(2,128)(2,1)S(1)} %reshape.11), channel_id=1, replica_groups=mesh['x'=4,'z'=16,'c'=2,'y'=4] {'z'}, dimensions={0} | all-to-all | bytes 24576 | tf_op jit(solution)/shard_map/all_to_all | solution.py:209
  82.0 0.1 reshape.12.arrived
  82.1 0.0 copy-start.6
  82.1 0.9 copy-done.6
  83.0 0.9 shard_map.143
  83.9 12.7 %all_to_all.48.arrived = bf16[32,16,128]{2,1,0:T(8,128)(2,1)S(1)} all-to-all(bf16[32,16,128]{2,1,0:T(8,128)(2,1)S(1)} %get-tuple-element.8), channel_id=1, replica_groups=mesh['x'=4,'z'=16,'c'=2,'y'=4] {'x','c','y'}, dimensions={0} | all-to-all | bytes 262144 | tf_op jit(solution)/shard_map/all_to_all | solution.py:209
  96.7 14.2 %all_to_all.49.arrived = bf16[16,16,128]{2,1,0:T(8,128)(2,1)S(1)} all-to-all(bf16[16,16,128]{2,1,0:T(8,128)(2,1)S(1)} %shard_map.144), channel_id=1, replica_groups=mesh['x'=4,'z'=16,'c'=2,'y'=4] {'z'}, dimensions={0} | all-to-all | bytes 131072 | tf_op jit(solution)/shard_map/all_to_all | solution.py:209
  110.9 0.7 shard_map.145
  111.6 5.5 %all-to-all-start.6 = ((bf16[32,16,128]{2,1,0:T(8,128)(2,1)}), bf16[32,16,128]{2,1,0:T(8,128)(2,1)S(1)}, u32[]{:S(2)}, u32[]{:S(2)}) async-start(bf16[32,16,128]{2,1,0:T(8,128)(2,1)} %shard_map.145), calls=%async_computation.6 | async-start | bytes 262144 | tf_op jit(solution)/shard_map/all_to_all | solution.py:209
  117.1 0.7 reshape.8.gain
  117.9 0.0 copy-done.8
  117.9 0.1 copy.15.expert_ids
  117.9 0.8 copy.16.route_weights
  118.7 6.1 %all-to-all-done.6.mid_blocks = bf16[32,16,128]{2,1,0:T(8,128)(2,1)S(1)} async-done(((bf16[32,16,128]{2,1,0:T(8,128)(2,1)}), bf16[32,16,128]{2,1,0:T(8,128)(2,1)S(1)}, u32[]{:S(2)}, u32[]{:S(2)}) %all-to-all-start.6) | async-done | bytes 131104 | tf_op jit(solution)/shard_map/all_to_all | solution.py:209
  124.8 0.0 copy-done
  124.8 0.0 copy-done.1
  124.8 0.0 copy-start.2
  124.8 1.2 copy-done.2
  126.1 0.0 copy-start.3
  126.1 1.2 copy-done.3
  127.3 2.5 %shard_map.146 = bf16[32,16,128]{2,1,0:T(8,128)(2,1)S(1)} custom-call(s32[5]{0:T(128)S(1)} %stack.23.place, bf16[32,16,128]{2,1,0:T(8,128)(2,1)S(1)} %all-to-all-done.6.mid_blocks, bf16[1,4096]{1,0:T(2,128)(2,1)S(1)} %reshape.8.gain, s32[16,8]{1,0:T(8,128)S(1)} %copy.15.expert_ids, f32[16,8]{1,0:T(8,128)S(1)} %copy.16.route_weights, ...), custom_call_target="tpu_custom_call" | custom-call | tf_op jit(solution)/shard_map/pallas_call | solution.py:198
  129.8 11.4 %all_to_all.50.arrived = bf16[32,16,128]{2,1,0:T(8,128)(2,1)S(1)} all-to-all(bf16[32,16,128]{2,1,0:T(8,128)(2,1)S(1)} %shard_map.146), channel_id=1, replica_groups=mesh['x'=4,'z'=16,'c'=2,'y'=4] {'x','c','y'}, dimensions={0} | all-to-all | bytes 262144 | tf_op jit(solution)/shard_map/all_to_all | solution.py:209
  141.2 0.2 shard_map.147
  141.3 14.0 %all_to_all.51.arrived = bf16[16,8,16]{2,1,0:T(8,128)(2,1)S(1)} all-to-all(bf16[16,8,16]{2,1,0:T(8,128)(2,1)S(1)} %shard_map.147), channel_id=1, replica_groups=mesh['x'=4,'z'=16,'c'=2,'y'=4] {'z'}, dimensions={0} | all-to-all | bytes 8192 | tf_op jit(solution)/shard_map/all_to_all | solution.py:209
  155.3 0.7 shard_map.148
  156.0 0.7 copy.17
  (2 shorter events, 0.0 us)
Async XLA Ops:
  30.2 87.7 %copy-start.8 = (s32[16,8]{0,1:T(8,128)S(1)}, s32[16,8]{0,1:T(8,128)}, u32[]{:S(2)}) copy-start(s32[16,8]{0,1:T(8,128)} %param.20) | copy-start | bytes 1540
  30.2 19.3 %all-to-all-start.1 = ((bf16[32,48,128]{2,1,0:T(8,128)(2,1)}), bf16[32,48,128]{2,1,0:T(8,128)(2,1)S(1)}, u32[]{:S(2)}, u32[]{:S(2)}) async-start(bf16[32,48,128]{2,1,0:T(8,128)(2,1)} %shard_map.140), calls=%async_computation.1 | async-start | bytes 786432 | tf_op jit(solution)/shard_map/all_to_all | solution.py:209
  39.5 85.3 %copy-start = (bf16[1024,1024]{1,0:T(8,128)(2,1)S(1)}, bf16[1024,1024]{1,0:T(8,128)(2,1)}, u32[]{:S(2)}) copy-start(bf16[1024,1024]{1,0:T(8,128)(2,1)} %constant.26.clone.order) | copy-start | bytes 6291460
  39.5 85.3 %copy-start.1 = (bf16[128,4096]{1,0:T(8,128)(2,1)S(1)}, bf16[128,4096]{1,0:T(8,128)(2,1)}, u32[]{:S(2)}) copy-start(bf16[128,4096]{1,0:T(8,128)(2,1)} %w_gate.1) | copy-start | bytes 3145732
  49.5 1.0 copy-start.4
  50.6 1.0 copy-start.5
  51.6 0.7 copy-start.7
  82.1 0.9 copy-start.6
  111.6 13.2 %all-to-all-start.6 = ((bf16[32,16,128]{2,1,0:T(8,128)(2,1)}), bf16[32,16,128]{2,1,0:T(8,128)(2,1)S(1)}, u32[]{:S(2)}, u32[]{:S(2)}) async-start(bf16[32,16,128]{2,1,0:T(8,128)(2,1)} %shard_map.145), calls=%async_computation.6 | async-start | bytes 262144 | tf_op jit(solution)/shard_map/all_to_all | solution.py:209
  124.8 1.2 copy-start.2
  126.1 1.2 copy-start.3

commit v2 on v1

v2 whole, which is shorter than its diff:
```python
import math

import jax
import jax.numpy as jnp
import numpy as np
from jax import lax
from jax.experimental import pallas as pl
from jax.experimental.pallas import tpu as pltpu
from jax.sharding import Mesh
from jax.sharding import PartitionSpec as P

HD = 128
X, Z, CY = 4, 16, 8
PLANE = X * CY
B = 16
D = 4096
COLS = D // Z
SPAN = 32
FLOOR = -1e30
BF = jnp.bfloat16
F32 = jnp.float32
PLANE_AXES = ("x", "c", "y")
ALL_AXES = ("x", "z", "c", "y")
EXACT = lax.Precision.HIGHEST


def iota(shape, dimension):
    return lax.broadcasted_iota(jnp.int32, shape, dimension)


def dot(a, b, dims, precision=None):
    return lax.dot_general(
        a, b, (dims, ((), ())), preferred_element_type=F32, precision=precision
    )


def eye(n, dtype=BF):
    return (iota((n, n), 0) == iota((n, n), 1)).astype(dtype)


def halves(first, second, high):
    low_lanes = iota(first.shape, 1) < 64
    if high:
        return jnp.where(low_lanes, pltpu.roll(first, 64, 1), second)
    return jnp.where(low_lanes, first, pltpu.roll(second, 64, 1))


def deal_out(query, out_proj, out, held, sem):
    copy = pltpu.make_async_copy(out_proj, held, sem)
    copy.start()
    place = (iota((16, 128), 0) == iota((16, 128), 1)).astype(BF)
    wide = dot(query[...], place, ((1,), (0,))).astype(BF)
    copy.wait()
    for v in range(Z // 2):
        tiles = [
            held[:, x * 1024 + v * 128 : x * 1024 + (v + 1) * 128].astype(F32) for x in range(X)
        ]
        for high in range(2):
            z = 2 * v + high
            out[z, :, 0:128] = halves(tiles[0], tiles[1], high).astype(BF)
            out[z, :, 128:256] = halves(tiles[2], tiles[3], high).astype(BF)
            out[z, :, 256:384] = wide


def spread_query(arrived, out):
    rows = arrived[:, :, 256:384].astype(F32)
    unit = eye(128)
    parts = []
    for i in range(2):
        part = rows[:, i * 8 : (i + 1) * 8, :].reshape(128, 128).astype(BF)
        parts.append(dot(part, unit, ((0,), (0,)))[:16])
    turned = jnp.concatenate(parts, axis=0).astype(BF)
    for k in range(PLANE):
        out[k] = turned


def attend(place, lengths, gathered, hidden, keys, values, out, held_keys, held_values, sems):
    copies = []
    for i in range(2):
        part = pl.ds(i * 8, 8)
        copies.append(
            [
                pltpu.make_async_copy(keys.at[part], held_keys.at[part], sems.at[i, 0]),
                pltpu.make_async_copy(values.at[part], held_values.at[part], sems.at[i, 1]),
            ]
        )
        for copy in copies[i]:
            copy.start()
    device = place[0]
    lane_j = iota((SPAN, 128), 1) % 8
    position = device * SPAN + iota((SPAN, 128), 0)
    spot = (iota((B, 128), 0) == iota((B, 128), 1) % B).astype(BF)
    repeated = dot(hidden[...], spot, ((1,), (0,)))
    own = jnp.where(iota((8, 128), 0) == iota((8, 128), 1) // B, repeated, 0.0)
    own = jnp.sum(own, axis=0, keepdims=True)
    zeros = jnp.zeros((9, 128), F32)
    stats = [[None] * 6 for _ in range(X)]
    for i in range(2):
        valid = jnp.concatenate(
            [
                ((lane_j == j) & (position < lengths[i * 8 + j])).astype(F32)
                for j in range(8)
            ],
            axis=0,
        )
        valid = valid > 0.5
        copies[i][0].wait()
        copies[i][1].wait()
        for g in range(X):
            query = gathered[g * CY : (g + 1) * CY, i * 16 : (i + 1) * 16, :].reshape(HD, 128)
            k = held_keys[i * 8 : (i + 1) * 8, :, g * HD : (g + 1) * HD].reshape(8 * SPAN, HD)
            v = held_values[i * 8 : (i + 1) * 8, :, g * HD : (g + 1) * HD].reshape(8 * SPAN, HD)
            scores = dot(k, query, ((1,), (0,))) * (1.0 / math.sqrt(HD))
            scores = jnp.where(valid, scores, FLOOR)
            top = jnp.max(scores, axis=0, keepdims=True).astype(BF).astype(F32)
            weights = jnp.where(valid, jnp.exp(scores - top), 0.0).astype(BF)
            total = jnp.sum(weights.astype(F32), axis=0, keepdims=True)
            mixed = dot(v, weights, ((0,), (0,))).astype(BF)
            for c in range(CY):
                out[g * CY + c, i * 16 : (i + 1) * 16, :] = mixed[c * 16 : (c + 1) * 16]
            high = total.astype(BF).astype(F32)
            stats[g][i] = top
            stats[g][2 + i] = high
            stats[g][4 + i] = total - high
    for g in range(X):
        block = jnp.concatenate(stats[g] + [own, zeros], axis=0).astype(BF)
        for c in range(CY):
            out[g * CY + c, 32:48, :] = block


def merge(arrived, i):
    top = arrived[:, 32 + i, :].astype(F32)
    total = arrived[:, 34 + i, :].astype(F32) + arrived[:, 36 + i, :].astype(F32)
    best = jnp.max(top, axis=0, keepdims=True)
    scale = jnp.exp(top - best)
    mass = jnp.sum(total * scale, axis=0, keepdims=True)
    mixed = arrived[:, i * 16 : (i + 1) * 16, :].astype(F32)
    return jnp.sum(mixed * scale[:, None, :], axis=0), best, mass


def merge_plane(arrived, out, hidden_cols):
    parts, tops, highs, lows = [], [], [], []
    for i in range(2):
        mixed, best, mass = merge(arrived, i)
        high = mass.astype(BF).astype(F32)
        parts.append(mixed)
        tops.append(best)
        highs.append(high)
        lows.append(mass - high)
    full = jnp.concatenate(
        parts + tops + highs + lows + [jnp.zeros((10, 128), F32)], axis=0
    ).astype(BF)
    for z in range(Z):
        out[z] = full
    owned = arrived[:, 38, :].astype(F32).astype(BF)
    for t in range(2):
        put = (iota((16, 128), 0) == iota((16, 128), 1) // 8).astype(BF)
        by_lane = dot(owned[t * 16 : (t + 1) * 16], put, ((0,), (0,)))
        mine = iota((128, 128), 0) // B == iota((128, 128), 1) % 8
        by_lane = jnp.where(mine, by_lane, 0.0).reshape(8, B, 128)
        hidden_cols[:, t * 128 : (t + 1) * 128] = jnp.sum(by_lane, axis=0)


def finish_context(place, arrived, dealt, context, out):
    z = place[2]
    weights = dealt[:, :, 0:COLS].reshape(Z * 16, COLS)
    contexts, terms = [], []
    for i in range(2):
        mixed, _, mass = merge(arrived, i)
        done = (mixed / mass).astype(BF)
        mine = (iota((8, 128), 1) == z * 8 + iota((8, 128), 0)).astype(BF)
        contexts.append(dot(mine, done, ((1,), (1,))))
        tile = (iota((16, 256), 0) == iota((16, 256), 1) % 16).astype(BF)
        tiled = dot(done, tile, ((0,), (0,)))
        block = iota((128, 256), 0) // 8 == iota((128, 256), 1) // 16
        tiled = jnp.where(block, tiled, 0.0).astype(BF)
        term = dot(tiled, weights, ((1,), (0,)))
        terms.append(jnp.sum(term.reshape(Z, 8, COLS), axis=0))
    context[...] = jnp.concatenate(contexts, axis=0).astype(BF)
    term = jnp.concatenate(terms, axis=0).astype(BF)
    for k in range(PLANE):
        out[k] = term


def slots(ids, expert, rows):
    hits = jnp.zeros((rows, B), F32)
    for k in range(8):
        hits += (ids[k : k + 1, :] == expert).astype(F32)
    before = (iota((B, B), 0) < iota((B, B), 1)).astype(BF)
    rank = dot(hits.astype(BF), before, ((1,), (0,)))
    return (hits > 0.5) & (jnp.abs(rank - (iota((rows, B), 0) % 8).astype(F32)) < 0.5)


def make_mid(place, arrived, hidden_cols, expert_ids, out, mid_part):
    x, cy = place[1], place[3]
    projected = jnp.sum(arrived[...].astype(F32), axis=0)
    mid = (projected + hidden_cols[...]).astype(BF)
    expert = x * Z + iota((128, B), 0) // 8
    table = slots(expert_ids[...], expert, 128).astype(BF)
    picked = dot(table, mid, ((1,), (0,)))
    parts = [picked[:, t * 128 : (t + 1) * 128].reshape(Z, 8, 128) for t in range(2)]
    out[...] = jnp.concatenate(parts, axis=1).astype(BF)
    mine = iota((8, COLS), 1) == x * 64 + cy * 8 + iota((8, COLS), 0)
    mid_part[...] = dot(mine.astype(BF), mid, ((1,), (1,)))


def experts(
    place, arrived, gain, expert_ids, route_weights, w_gate, order, w_up, w_down, out,
    held_up, held_down, sems,
):
    up_copy = pltpu.make_async_copy(w_up, held_up, sems.at[0])
    down_copy = pltpu.make_async_copy(w_down, held_down, sems.at[1])
    up_copy.start()
    down_copy.start()
    expert = place[4]
    ids = expert_ids[...]
    routes = route_weights[...]
    table = slots(ids, expert, 8)
    share = routes / jnp.sum(routes, axis=0, keepdims=True)
    weight = jnp.sum(jnp.where(ids == expert, share, 0.0), axis=0, keepdims=True)
    coefficient = jnp.sum(jnp.where(table, weight, 0.0), axis=1, keepdims=True)
    table = table.astype(BF)
    tiles = []
    for x in range(X):
        t = x // 2
        for v in range(Z // 2):
            first = arrived[2 * v].astype(F32)[t * 8 : (t + 1) * 8]
            second = arrived[2 * v + 1].astype(F32)[t * 8 : (t + 1) * 8]
            tiles.append(halves(first, second, x % 2))
    rows = jnp.concatenate(tiles, axis=1)
    scale = lax.rsqrt(jnp.sum(rows * rows, axis=1, keepdims=True) * (1.0 / D) + 1e-06)
    picked = (rows * scale * gain[...].astype(F32)).astype(BF)
    gate = dot(picked, w_gate[...], ((1,), (1,)))
    up_copy.wait()
    upward = dot(picked, held_up[...], ((1,), (1,)))
    hidden_units = (gate / (1.0 + jnp.exp(-gate)) * upward).astype(BF)
    down_copy.wait()
    weighted = (dot(hidden_units, held_down[...], ((1,), (0,))) * coefficient).astype(BF)
    back = dot(table, weighted, ((0,), (0,))).astype(BF)
    stacked = jnp.concatenate([back[:, x * 1024 : (x + 1) * 1024] for x in range(X)], axis=0)
    sorted_back = dot(stacked, order[...], ((1,), (0,))).astype(BF)
    for x in range(X):
        for c in range(CY):
            out[x * CY + c] = sorted_back[x * B : (x + 1) * B, c * 128 : (c + 1) * 128]


def sum_experts(arrived, out):
    total = jnp.sum(arrived[...].astype(F32), axis=0).astype(BF)
    turned = dot(eye(128), total, ((1,), (1,)))
    out[...] = turned.reshape(Z, 8, B).astype(BF)


def finish_layer(arrived, mid_part, out):
    out[...] = (mid_part[...] + jnp.sum(arrived[...].astype(F32), axis=0)).astype(BF)


def call(body, outs, scalars, arrays, far=(), scratch=()):
    smem = pl.BlockSpec(memory_space=pltpu.SMEM)
    vmem = pl.BlockSpec(memory_space=pltpu.VMEM)
    anywhere = pl.BlockSpec(memory_space=pl.ANY)
    single = not isinstance(outs, list)
    return pl.pallas_call(
        body,
        out_shape=outs,
        in_specs=[smem] * len(scalars) + [vmem] * len(arrays) + [anywhere] * len(far),
        out_specs=vmem if single else [vmem] * len(outs),
        scratch_shapes=list(scratch),
        compiler_params=pltpu.CompilerParams(vmem_limit_bytes=24 * 1024 * 1024),
    )(*scalars, *arrays, *far)


def swap(blocks, axes):
    return lax.all_to_all(blocks, axes, 0, 0, tiled=True)


def block_order():
    columns = np.arange(1024).reshape(Z, CY, 8).transpose(1, 0, 2).reshape(-1)
    order = np.zeros((1024, 1024), np.float32)
    order[columns, np.arange(1024)] = 1.0
    return order.astype(jnp.bfloat16)


def shards(
    query,
    key_cache,
    value_cache,
    lengths,
    hidden_in,
    out_proj,
    norm_gain,
    expert_ids,
    route_weights,
    w_gate,
    w_up,
    w_down,
):
    x, z = lax.axis_index("x"), lax.axis_index("z")
    cy = lax.axis_index("c") * 4 + lax.axis_index("y")
    expert = x * Z + z
    place = jnp.stack([expert * CY + cy, x, z, cy, expert]).astype(jnp.int32)
    ids, routes = expert_ids.T, route_weights.T
    dma = pltpu.SemaphoreType.DMA

    def shape(*dims, dtype=BF):
        return jax.ShapeDtypeStruct(dims, dtype)

    dealt = swap(
        call(
            deal_out,
            shape(Z, 16, COLS + 128),
            (),
            (query,),
            (out_proj,),
            (pltpu.VMEM((16, D), BF), dma),
        ),
        "z",
    )
    gathered = swap(call(spread_query, shape(PLANE, 32, 128), (), (dealt,)), PLANE_AXES)
    partial = call(
        attend,
        shape(PLANE, 48, 128),
        (place, lengths),
        (gathered, hidden_in.T),
        (key_cache, value_cache),
        (pltpu.VMEM((B, SPAN, 512), BF), pltpu.VMEM((B, SPAN, 512), BF), dma((2, 2))),
    )
    merged, hidden_cols = call(
        merge_plane,
        [shape(Z, 48, 128), shape(B, COLS, dtype=F32)],
        (),
        (swap(partial, PLANE_AXES),),
    )
    context, term = call(
        finish_context,
        [shape(B, 16), shape(PLANE, B, COLS)],
        (place,),
        (swap(merged, "z"), dealt),
    )
    picked, mid_part = call(
        make_mid,
        [shape(Z, 16, 128), shape(8, B, dtype=F32)],
        (place,),
        (swap(term, PLANE_AXES), hidden_cols, ids),
    )
    mixture = call(
        experts,
        shape(PLANE, B, 128),
        (place,),
        (
            swap(picked, "z"),
            norm_gain.reshape(1, D),
            ids,
            routes,
            w_gate,
            jnp.asarray(block_order()),
        ),
        (w_up, w_down),
        (pltpu.VMEM((128, D), BF), pltpu.VMEM((128, D), BF), dma((2,))),
    )
    summed = call(sum_experts, shape(Z, 8, B), (), (swap(mixture, PLANE_AXES),))
    layer_out = call(finish_layer, shape(8, B), (), (swap(summed, "z"), mid_part))
    return context, layer_out.T


def solution(mesh):
    fine = Mesh(np.asarray(mesh.devices).reshape(X, Z, 2, 4), ALL_AXES)
    columns, rows = P(None, ALL_AXES), P(ALL_AXES, None)
    cache = P(None, ALL_AXES, None)
    placed = (
        columns,
        cache,
        cache,
        P(),
        columns,
        rows,
        P(),
        P(),
        P(),
        rows,
        rows,
        rows,
    )
    return jax.shard_map(
        shards,
        mesh=fine,
        in_specs=placed,
        out_specs=(columns, columns),
        check_vma=False,
    )
```

time: 158 us -> 158 us (level)
  waiting for transfers between devices: 16 us -> 20.2 us
  blocking collectives: 107 us -> 103 us
  local copies, waits for them, and re-layouts: 9.54 us -> 6.58 us
  Pallas kernels: 7.71 us -> 10 us
  starting transfers between devices: 14.8 us -> 16.6 us
    all_to_all x2, waiting for transfers between devices: 16 us -> 20.2 us  [swap(): return lax.all_to_all(blocks, axes, 0, 0, tiled=True)]
    all_to_all x7 -> x6, blocking collectives: 107 us -> 103 us  [swap(): return lax.all_to_all(blocks, axes, 0, 0, tiled=True)]
    pallas_call x9, Pallas kernels: 7.71 us -> 10 us  [call(): pl.pallas_call(body, out_shape=outs, in_specs=[smem] * len(scalars) + [vm...]
    all_to_all x2, starting transfers between devices: 14.8 us -> 16.6 us  [swap(): return lax.all_to_all(blocks, axes, 0, 0, tiled=True)]
    unnamed x25 -> x26, local copies, waits for them, and re-layouts: 8.04 us -> 6.49 us
  transfers between devices with their start and end apart: 2 -> 2, of which waited for: 2 -> 2; matrix products, arithmetic and copies ran while one was open for 1% -> 0% of each run, Pallas kernels for 0% -> 0%
where the time goes in v2:
time: 158 us; the launch traced here: 157 us
  blocking collectives  103 us (65%)
  waiting for transfers between devices  20.2 us (13%)
  starting transfers between devices  16.6 us (11%)
  Pallas kernels  10 us (6%)
  local copies, waits for them, and re-layouts  6.58 us (4%)
    all_to_all x6, blocking collectives, swap(): return lax.all_to_all(blocks, axes, 0, 0, tiled=True)  103 us
    all_to_all x2, waiting for transfers between devices, swap(): return lax.all_to_all(blocks, axes, 0, 0, tiled=True)  20.2 us
    all_to_all x2, starting transfers between devices, swap(): return lax.all_to_all(blocks, axes, 0, 0, tiled=True)  16.6 us
    pallas_call x9, Pallas kernels, call(): pl.pallas_call(body, out_shape=outs, in_specs=[smem] * len(scalars) + [vm...  10 us
    unnamed x26, local copies, waits for them, and re-layouts  6.49 us
  transfers between devices with their start and end apart: 2, of which 2 were waited for; matrix products, arithmetic and copies ran while one was open for 0% of the time, Pallas kernels for 0%

profile of v2, /device:TPU:1, one launch (start us, length us, event | category | flops | bytes accessed | tf_op | source)
XLA Modules:
  0.0 157.1 jit_solution(2891005239659750308)
XLA Ops:
  0.6 0.0 copy-start.4
  0.6 0.0 copy-start.6
  0.6 1.0 copy-done.6
  1.6 0.0 copy-start.8
  1.6 0.7 copy-done.8
  2.3 0.4 shard_map.140
  2.7 28.1 %all_to_all.40.arrived.dealt = bf16[16,16,384]{2,1,0:T(8,128)(2,1)S(1)} all-to-all(bf16[16,16,384]{2,1,0:T(8,128)(2,1)S(1)} %shard_map.140), channel_id=1, replica_groups=mesh['x'=4,'z'=16,'c'=2,'y'=4] {'z'}, dimensions={0} | all-to-all | bytes 393216 | tf_op jit(solution)/shard_map/all_to_all | solution.py:273
  30.8 0.9 shard_map.141
  31.7 11.9 %all-to-all-start.1 = ((bf16[32,32,128]{2,1,0:T(8,128)(2,1)}), bf16[32,32,128]{2,1,0:T(8,128)(2,1)S(1)}, u32[]{:S(2)}, u32[]{:S(2)}) async-start(bf16[32,32,128]{2,1,0:T(8,128)(2,1)} %shard_map.141), calls=%async_computation.1 | async-start | bytes 524288 | tf_op jit(solution)/shard_map/all_to_all | solution.py:273
  43.6 0.1 stack.23.place
  43.7 8.7 %all-to-all-done.1.gathered = bf16[32,32,128]{2,1,0:T(8,128)(2,1)S(1)} async-done(((bf16[32,32,128]{2,1,0:T(8,128)(2,1)}), bf16[32,32,128]{2,1,0:T(8,128)(2,1)S(1)}, u32[]{:S(2)}, u32[]{:S(2)}) %all-to-all-start.1) | async-done | bytes 262176 | tf_op jit(solution)/shard_map/all_to_all | solution.py:273
  52.4 0.0 copy-done.4
  52.4 0.0 copy-start.5
  52.4 1.0 copy-done.5
  53.4 0.0 copy-start.10
  53.4 0.7 copy-done.10
  54.1 0.0 copy-start.11
  54.1 0.7 copy-done.11
  54.8 0.0 copy-start.7
  54.8 0.0 copy-start.12
  54.8 0.0 copy-start
  54.8 0.0 copy-start.9
  54.8 1.9 %shard_map.142 = bf16[32,48,128]{2,1,0:T(8,128)(2,1)S(1)} custom-call(s32[5]{0:T(128)S(1)} %stack.23.place, s32[16]{0:T(128)S(1)} %copy-done.11, bf16[32,32,128]{2,1,0:T(8,128)(2,1)S(1)} %all-to-all-done.1.gathered, bf16[8,16]{1,0:T(8,128)(2,1)S(1)} %bitcast.12, bf16[16,32,512]{2,1,0:T(8,128)(2,1)S(1)} %copy-done.4, bf16[16,32,512]{2,1,0:T(8,128)(2,1)S(1)} %copy-done.5), custom_call_target="tpu_custom_call" | custom-call | tf_op jit(solution)/shard_map/pallas_call | solution.py:262
  56.7 0.0 copy-start.1
  56.7 14.1 %all_to_all.41.arrived = bf16[32,48,128]{2,1,0:T(8,128)(2,1)S(1)} all-to-all(bf16[32,48,128]{2,1,0:T(8,128)(2,1)S(1)} %shard_map.142), channel_id=1, replica_groups=mesh['x'=4,'z'=16,'c'=2,'y'=4] {'x','c','y'}, dimensions={0} | all-to-all | bytes 786432 | tf_op jit(solution)/shard_map/all_to_all | solution.py:273
  70.8 0.3 shard_map.143
  71.1 17.0 %all_to_all.42.arrived = bf16[16,48,128]{2,1,0:T(8,128)(2,1)S(1)} all-to-all(bf16[16,48,128]{2,1,0:T(8,128)(2,1)S(1)} %get-tuple-element.8), channel_id=1, replica_groups=mesh['x'=4,'z'=16,'c'=2,'y'=4] {'z'}, dimensions={0} | all-to-all | bytes 393216 | tf_op jit(solution)/shard_map/all_to_all | solution.py:273
  88.1 1.3 shard_map.144
  89.4 16.7 %all_to_all.43.arrived = bf16[32,16,256]{2,1,0:T(8,128)(2,1)S(1)} all-to-all(bf16[32,16,256]{2,1,0:T(8,128)(2,1)S(1)} %get-tuple-element.10), channel_id=1, replica_groups=mesh['x'=4,'z'=16,'c'=2,'y'=4] {'x','c','y'}, dimensions={0} | all-to-all | bytes 524288 | tf_op jit(solution)/shard_map/all_to_all | solution.py:273
  106.1 0.0 copy-done.7
  106.2 1.5 shard_map.145
  107.6 4.6 %all-to-all-start.5 = ((bf16[16,16,128]{2,1,0:T(8,128)(2,1)}), bf16[16,16,128]{2,1,0:T(8,128)(2,1)S(1)}, u32[]{:S(2)}, u32[]{:S(2)}) async-start(bf16[16,16,128]{2,1,0:T(8,128)(2,1)} %get-tuple-element.12), calls=%async_computation.5 | async-start | bytes 131072 | tf_op jit(solution)/shard_map/all_to_all | solution.py:273
  112.3 0.0 copy-done.12
  112.3 11.5 %all-to-all-done.5.arrived = bf16[16,16,128]{2,1,0:T(8,128)(2,1)S(1)} async-done(((bf16[16,16,128]{2,1,0:T(8,128)(2,1)}), bf16[16,16,128]{2,1,0:T(8,128)(2,1)S(1)}, u32[]{:S(2)}, u32[]{:S(2)}) %all-to-all-start.5) | async-done | bytes 65568 | tf_op jit(solution)/shard_map/all_to_all | solution.py:273
  123.8 0.0 copy-done
  123.8 0.0 copy-done.9
  123.8 0.0 copy-done.1
  123.8 0.0 copy-start.2
  123.9 1.2 copy-done.2
  125.1 0.0 copy-start.3
  125.1 1.2 copy-done.3
  126.3 2.9 %shard_map.146 = bf16[32,16,128]{2,1,0:T(8,128)(2,1)S(1)} custom-call(s32[5]{0:T(128)S(1)} %stack.23.place, bf16[16,16,128]{2,1,0:T(8,128)(2,1)S(1)} %all-to-all-done.5.arrived, bf16[1,4096]{1,0:T(2,128)(2,1)S(1)} %reshape.7.gain, s32[8,16]{1,0:T(8,128)S(1)} %bitcast.10, f32[8,16]{1,0:T(8,128)S(1)} %bitcast.11, bf16[128,4096]{1,0:T(8,128)(2,1)S(1)} %copy-done.1, ...), custom_call_target="tpu_custom_call" | custom-call | tf_op jit(solution)/shard_map/pallas_call | solution.py:262
  129.3 13.1 %all_to_all.44.arrived = bf16[32,16,128]{2,1,0:T(8,128)(2,1)S(1)} all-to-all(bf16[32,16,128]{2,1,0:T(8,128)(2,1)S(1)} %shard_map.146), channel_id=1, replica_groups=mesh['x'=4,'z'=16,'c'=2,'y'=4] {'x','c','y'}, dimensions={0} | all-to-all | bytes 262144 | tf_op jit(solution)/shard_map/all_to_all | solution.py:273
  142.3 0.2 shard_map.147
  142.5 14.0 %all_to_all.45.arrived = bf16[16,8,16]{2,1,0:T(8,128)(2,1)S(1)} all-to-all(bf16[16,8,16]{2,1,0:T(8,128)(2,1)S(1)} %shard_map.147), channel_id=1, replica_groups=mesh['x'=4,'z'=16,'c'=2,'y'=4] {'z'}, dimensions={0} | all-to-all | bytes 8192 | tf_op jit(solution)/shard_map/all_to_all | solution.py:273
  156.5 0.6 shard_map.148
  (1 shorter events, 0.0 us)
Async XLA Ops:
  0.6 51.8 %copy-start.4 = (bf16[16,32,512]{2,1,0:T(8,128)(2,1)S(1)}, bf16[16,32,512]{2,1,0:T(8,128)(2,1)}, u32[]{:S(2)}) copy-start(bf16[16,32,512]{2,1,0:T(8,128)(2,1)} %keys.1) | copy-start | bytes 1572868
  0.6 1.0 copy-start.6
  1.6 0.7 copy-start.8
  31.7 20.7 %all-to-all-start.1 = ((bf16[32,32,128]{2,1,0:T(8,128)(2,1)}), bf16[32,32,128]{2,1,0:T(8,128)(2,1)S(1)}, u32[]{:S(2)}, u32[]{:S(2)}) async-start(bf16[32,32,128]{2,1,0:T(8,128)(2,1)} %shard_map.141), calls=%async_computation.1 | async-start | bytes 524288 | tf_op jit(solution)/shard_map/all_to_all | solution.py:273
  52.4 1.0 copy-start.5
  53.4 0.7 copy-start.10
  54.1 0.7 copy-start.11
  54.8 51.4 %copy-start.7 = (s32[16,8]{0,1:T(8,128)S(1)}, s32[16,8]{0,1:T(8,128)}, u32[]{:S(2)}) copy-start(s32[16,8]{0,1:T(8,128)} %param.20) | copy-start | bytes 1540
  54.8 57.5 %copy-start.12 = (bf16[4096]{0:T(1024)(128)(2,1)S(1)}, bf16[4096]{0:T(1024)(128)(2,1)}, u32[]{:S(2)}) copy-start(bf16[4096]{0:T(1024)(128)(2,1)} %param.19) | copy-start | bytes 24580
  54.8 69.1 %copy-start = (bf16[1024,1024]{1,0:T(8,128)(2,1)S(1)}, bf16[1024,1024]{1,0:T(8,128)(2,1)}, u32[]{:S(2)}) copy-start(bf16[1024,1024]{1,0:T(8,128)(2,1)} %constant.26.clone.order) | copy-start | bytes 6291460
  54.8 69.1 %copy-start.9 = (f32[16,8]{0,1:T(8,128)S(1)}, f32[16,8]{0,1:T(8,128)}, u32[]{:S(2)}) copy-start(f32[16,8]{0,1:T(8,128)} %param.21) | copy-start | bytes 1540
  56.7 67.2 %copy-start.1 = (bf16[128,4096]{1,0:T(8,128)(2,1)S(1)}, bf16[128,4096]{1,0:T(8,128)(2,1)}, u32[]{:S(2)}) copy-start(bf16[128,4096]{1,0:T(8,128)(2,1)} %w_gate.1) | copy-start | bytes 3145732
  107.6 16.2 %all-to-all-start.5 = ((bf16[16,16,128]{2,1,0:T(8,128)(2,1)}), bf16[16,16,128]{2,1,0:T(8,128)(2,1)S(1)}, u32[]{:S(2)}, u32[]{:S(2)}) async-start(bf16[16,16,128]{2,1,0:T(8,128)(2,1)} %get-tuple-element.12), calls=%async_computation.5 | async-start | bytes 131072 | tf_op jit(solution)/shard_map/all_to_all | solution.py:273
  123.8 1.2 copy-start.2
  125.1 1.2 copy-start.3

commit v3 on v2

v3 whole, which is shorter than its diff:
```python
import math

import jax
import jax.numpy as jnp
import numpy as np
from jax import lax
from jax.experimental import pallas as pl
from jax.experimental.pallas import tpu as pltpu
from jax.sharding import Mesh
from jax.sharding import PartitionSpec as P

HD = 128
X, Z, CY = 4, 16, 8
PLANE = X * CY
B = 16
D = 4096
COLS = D // Z
SPAN = 32
FLOOR = -1e30
BF = jnp.bfloat16
F32 = jnp.float32
PLANE_AXES = ("x", "c", "y")
ALL_AXES = ("x", "z", "c", "y")
EXACT = lax.Precision.HIGHEST


def iota(shape, dimension):
    return lax.broadcasted_iota(jnp.int32, shape, dimension)


def dot(a, b, dims, precision=None):
    return lax.dot_general(
        a, b, (dims, ((), ())), preferred_element_type=F32, precision=precision
    )


def eye(n, dtype=BF):
    return (iota((n, n), 0) == iota((n, n), 1)).astype(dtype)


def halves(first, second, high):
    low_lanes = iota(first.shape, 1) < 64
    if high:
        return jnp.where(low_lanes, pltpu.roll(first, 64, 1), second)
    return jnp.where(low_lanes, first, pltpu.roll(second, 64, 1))


def coordinates():
    x, z = lax.axis_index("x"), lax.axis_index("z")
    return x, z, lax.axis_index("c") * 4 + lax.axis_index("y")


def deal_out(query, out_proj, out, held_query, held, sems):
    copies = [
        pltpu.make_async_copy(query, held_query, sems.at[0]),
        pltpu.make_async_copy(out_proj, held, sems.at[1]),
    ]
    for copy in copies:
        copy.start()
    copies[0].wait()
    own = held_query[...]
    parts = []
    for i in range(2):
        put = (iota((16, 128), 0) + i * 16 == iota((16, 128), 1)).astype(BF)
        parts.append(dot(own, put, ((1,), (0,)))[i * 8 : (i + 1) * 8])
    wide = parts[0] + parts[1]
    copies[1].wait()
    for v in range(Z // 2):
        tiles = [
            held[:, x * 1024 + v * 128 : x * 1024 + (v + 1) * 128].astype(F32) for x in range(X)
        ]
        for high in range(2):
            pieces = [halves(tiles[0], tiles[1], high), halves(tiles[2], tiles[3], high), wide]
            out[2 * v + high] = jnp.concatenate(pieces, axis=0).astype(BF)


def spread_query(arrived, out):
    rows = arrived[:, 32:40, :].astype(F32).reshape(128, 128).astype(BF)
    turned = dot(rows, eye(128), ((0,), (0,)))[:32].astype(BF)
    for k in range(PLANE):
        out[k] = turned


def attend(gathered, keys, values, hidden, lengths, out, held_lengths, sem):
    copy = pltpu.make_async_copy(lengths, held_lengths, sem)
    copy.start()
    x, z, cy = coordinates()
    device = (x * Z + z) * CY + cy
    lane_j = iota((SPAN, 128), 1) % 8
    position = device * SPAN + iota((SPAN, 128), 0)
    spot = (iota((B, 128), 0) == iota((B, 128), 1) % B).astype(BF)
    repeated = dot(hidden[...], spot, ((1,), (0,)))
    own = jnp.where(iota((8, 128), 0) == iota((8, 128), 1) // B, repeated, 0.0)
    own = jnp.sum(own, axis=0, keepdims=True)
    zero = jnp.zeros((1, 128), F32)
    copy.wait()
    valids = []
    for i in range(2):
        rows = [(lane_j == j) & (position < held_lengths[i * 8 + j]) for j in range(8)]
        valids.append(jnp.concatenate([r.astype(F32) for r in rows], axis=0) > 0.5)
    for g in range(X):
        parts, tops, highs, lows = [], [], [], []
        for i in range(2):
            query = gathered[g * CY : (g + 1) * CY, i * 16 : (i + 1) * 16, :].reshape(HD, 128)
            k = keys[i * 8 : (i + 1) * 8, :, g * HD : (g + 1) * HD].reshape(8 * SPAN, HD)
            v = values[i * 8 : (i + 1) * 8, :, g * HD : (g + 1) * HD].reshape(8 * SPAN, HD)
            scores = dot(k, query, ((1,), (0,))) * (1.0 / math.sqrt(HD))
            scores = jnp.where(valids[i], scores, FLOOR)
            top = jnp.max(scores, axis=0, keepdims=True).astype(BF).astype(F32)
            weights = jnp.where(valids[i], jnp.exp(scores - top), 0.0).astype(BF)
            total = jnp.sum(weights.astype(F32), axis=0, keepdims=True)
            high = total.astype(BF).astype(F32)
            parts.append(dot(v, weights, ((0,), (0,))))
            tops.append(top)
            highs.append(high)
            lows.append(total - high)
        block = jnp.concatenate(tops + highs + lows + [own, zero], axis=0)
        for c in range(CY):
            pieces = [part[c * 16 : (c + 1) * 16] for part in parts]
            out[g * CY + c] = jnp.concatenate(pieces + [block], axis=0).astype(BF)


def merge(arrived, i):
    top = arrived[:, 32 + i, :].astype(F32)
    total = arrived[:, 34 + i, :].astype(F32) + arrived[:, 36 + i, :].astype(F32)
    best = jnp.max(top, axis=0, keepdims=True)
    scale = jnp.exp(top - best)
    mass = jnp.sum(total * scale, axis=0, keepdims=True)
    mixed = arrived[:, i * 16 : (i + 1) * 16, :].astype(F32)
    return jnp.sum(mixed * scale[:, None, :], axis=0), best, mass


def merge_plane(arrived, out, hidden_cols):
    parts, tops, highs, lows = [], [], [], []
    for i in range(2):
        mixed, best, mass = merge(arrived, i)
        high = mass.astype(BF).astype(F32)
        parts.append(mixed)
        tops.append(best)
        highs.append(high)
        lows.append(mass - high)
    full = jnp.concatenate(
        parts + tops + highs + lows + [jnp.zeros((2, 128), F32)], axis=0
    ).astype(BF)
    for z in range(Z):
        out[z] = full
    owned = arrived[:, 38, :].astype(F32).astype(BF)
    for t in range(2):
        put = (iota((16, 128), 0) == iota((16, 128), 1) // 8).astype(BF)
        by_lane = dot(owned[t * 16 : (t + 1) * 16], put, ((0,), (0,)))
        mine = iota((128, 128), 0) // B == iota((128, 128), 1) % 8
        by_lane = jnp.where(mine, by_lane, 0.0).reshape(8, B, 128)
        hidden_cols[:, t * 128 : (t + 1) * 128] = jnp.sum(by_lane, axis=0)


def finish_context(arrived, dealt, context, out):
    z = lax.axis_index("z")
    weights = jnp.concatenate(
        [dealt[:, t * 16 : (t + 1) * 16, :].reshape(Z * 16, 128) for t in range(2)], axis=1
    )
    contexts, terms = [], []
    for i in range(2):
        mixed, _, mass = merge(arrived, i)
        done = (mixed / mass).astype(BF)
        mine = (iota((8, 128), 1) == z * 8 + iota((8, 128), 0)).astype(BF)
        contexts.append(dot(mine, done, ((1,), (1,))))
        tile = (iota((16, 256), 0) == iota((16, 256), 1) % 16).astype(BF)
        tiled = dot(done, tile, ((0,), (0,)))
        block = iota((128, 256), 0) // 8 == iota((128, 256), 1) // 16
        tiled = jnp.where(block, tiled, 0.0).astype(BF)
        term = dot(tiled, weights, ((1,), (0,)))
        terms.append(jnp.sum(term.reshape(Z, 8, COLS), axis=0))
    context[...] = jnp.concatenate(contexts, axis=0).astype(BF)
    term = jnp.concatenate(terms, axis=0).astype(BF)
    for k in range(PLANE):
        out[k] = term


def slots(ids, expert, slot):
    hits = jnp.zeros(slot.shape, F32)
    for k in range(8):
        hits += (ids[k : k + 1, :] == expert).astype(F32)
    before = (iota((B, B), 0) < iota((B, B), 1)).astype(BF)
    rank = dot(hits.astype(BF), before, ((1,), (0,)))
    return (hits > 0.5) & (jnp.abs(rank - slot.astype(F32)) < 0.5)


def make_mid(arrived, hidden_cols, expert_ids, out, mid_part):
    x, _, cy = coordinates()
    projected = jnp.sum(arrived[...].astype(F32), axis=0)
    mid = (projected + hidden_cols[...]).astype(BF)
    row = iota((128, B), 0)
    table = slots(expert_ids[...], x * Z + row // 8, row % 4)
    picked = jnp.zeros((128, 128), F32)
    for t in range(2):
        half = (table & (row // 4 % 2 == t)).astype(BF)
        picked += dot(half, mid[:, t * 128 : (t + 1) * 128], ((1,), (0,)))
    out[...] = picked.reshape(Z, 8, 128).astype(BF)
    mine = iota((8, COLS), 1) == x * 64 + cy * 8 + iota((8, COLS), 0)
    mid_part[...] = dot(mine.astype(BF), mid, ((1,), (1,)))


def sort_columns(tiles):
    lane = iota((8, 128), 1)
    for bit in (32, 16, 8):
        low = lane // bit % 2 == 0
        high = lane // (2 * bit) % 2 == 0
        tiles = [
            jnp.where(
                low == high,
                tile,
                jnp.where(high, pltpu.roll(tile, 128 - bit, 1), pltpu.roll(tile, bit, 1)),
            )
            for tile in tiles
        ]
    for step in (4, 2, 1):
        low = lane // (16 * step) % 2 == 0
        swapped = list(tiles)
        for v in range(8):
            if v & step == 0:
                first, second = tiles[v], tiles[v + step]
                swapped[v] = jnp.where(low, first, pltpu.roll(second, 16 * step, 1))
                swapped[v + step] = jnp.where(low, pltpu.roll(first, 128 - 16 * step, 1), second)
        tiles = swapped
    return tiles


def experts(arrived, gain, expert_ids, route_weights, w_gate, w_up, w_down, out):
    x, z, _ = coordinates()
    expert = x * Z + z
    ids = expert_ids[...]
    routes = route_weights[...]
    table = slots(ids, expert, iota((8, B), 0))
    share = routes / jnp.sum(routes, axis=0, keepdims=True)
    weight = jnp.sum(jnp.where(ids == expert, share, 0.0), axis=0, keepdims=True)
    coefficient = jnp.sum(jnp.where(table, weight, 0.0), axis=1, keepdims=True)
    first_half = iota((8, 128), 0) < 4
    gains = gain[...].astype(F32)
    tiles, scaled = [], []
    for p in range(2):
        for v in range(Z // 2):
            tile = halves(arrived[2 * v].astype(F32), arrived[2 * v + 1].astype(F32), p)
            low, high = p * 8 + v, (2 + p) * 8 + v
            tiles.append(tile * tile)
            scaled.append(
                tile * jnp.where(first_half, gains[low : low + 1], gains[high : high + 1])
            )
    squares = sum(tiles[1:], tiles[0])
    squares = squares + jnp.concatenate([squares[4:], squares[:4]], axis=0)
    scale = lax.rsqrt(jnp.sum(squares, axis=1, keepdims=True) * (1.0 / D) + 1e-06)
    picked = jnp.concatenate([(tile * scale).astype(BF) for tile in scaled], axis=1)

    def project(weights):
        near = dot(picked, weights[:, : D // 2], ((1,), (1,)))
        far = dot(picked, weights[:, D // 2 :], ((1,), (1,)))
        return near + jnp.concatenate([far[4:], far[:4]], axis=0)

    gate = project(w_gate)
    upward = project(w_up)
    hidden_units = (gate / (1.0 + jnp.exp(-gate)) * upward).astype(BF)
    weighted = dot(hidden_units, w_down[...], ((1,), (0,))) * coefficient
    for group in range(X):
        start = group * 1024
        tiles = [weighted[:, start + v * 128 : start + (v + 1) * 128] for v in range(8)]
        for c, tile in enumerate(sort_columns(tiles)):
            out[group * CY + c] = tile.astype(BF)


def sum_experts(arrived, expert_ids, out):
    z = lax.axis_index("z")
    parts = [
        jnp.sum(arrived[x * CY : (x + 1) * CY].astype(F32), axis=0) for x in range(X)
    ]
    row = iota((8 * X, B), 0)
    table = slots(expert_ids[...], row // 8 * Z + z, row % 8).astype(F32)
    turned = dot(jnp.concatenate(parts, axis=0), table, ((0,), (0,)), EXACT)
    out[...] = turned.reshape(Z, 8, B).astype(BF)


def finish_layer(arrived, mid_part, out):
    out[...] = (mid_part[...] + jnp.sum(arrived[...].astype(F32), axis=0)).astype(BF)


def call(body, outs, arrays, far=(), scratch=(), limit=16):
    vmem = pl.BlockSpec(memory_space=pltpu.VMEM)
    remote = pl.BlockSpec(memory_space=pltpu.HBM)
    single = not isinstance(outs, list)
    return pl.pallas_call(
        body,
        out_shape=outs,
        in_specs=[vmem] * len(arrays) + [remote] * len(far),
        out_specs=vmem if single else [vmem] * len(outs),
        scratch_shapes=list(scratch),
        compiler_params=pltpu.CompilerParams(vmem_limit_bytes=limit * 1024 * 1024),
    )(*arrays, *far)


def swap(blocks, axes):
    return lax.all_to_all(blocks, axes, 0, 0, tiled=True)


def shards(
    query,
    key_cache,
    value_cache,
    lengths,
    hidden_in,
    out_proj,
    norm_gain,
    expert_ids,
    route_weights,
    w_gate,
    w_up,
    w_down,
):
    ids, routes = expert_ids.T, route_weights.T
    dma, vmem = pltpu.SemaphoreType.DMA, pltpu.VMEM

    def shape(*dims, dtype=BF):
        return jax.ShapeDtypeStruct(dims, dtype)

    dealt = swap(
        call(
            deal_out,
            shape(Z, 40, 128),
            (),
            (query, out_proj),
            (vmem((B, 16), BF), vmem((16, D), BF), dma((2,))),
            62,
        ),
        "z",
    )
    gathered = swap(call(spread_query, shape(PLANE, 32, 128), (dealt,)), PLANE_AXES)
    partial = call(
        attend,
        shape(PLANE, 40, 128),
        (gathered, key_cache, value_cache, hidden_in.T),
        (lengths,),
        (pltpu.SMEM((B,), jnp.int32), dma),
    )
    merged, hidden_cols = call(
        merge_plane,
        [shape(Z, 40, 128), shape(B, COLS, dtype=F32)],
        (swap(partial, PLANE_AXES),),
    )
    context, term = call(
        finish_context,
        [shape(B, 16), shape(PLANE, B, COLS)],
        (swap(merged, "z"), dealt),
    )
    picked, mid_part = call(
        make_mid,
        [shape(Z, 8, 128), shape(8, B, dtype=F32)],
        (swap(term, PLANE_AXES), hidden_cols, ids),
    )
    mixture = call(
        experts,
        shape(PLANE, 8, 128),
        (swap(picked, "z"), norm_gain.reshape(PLANE, 128), ids, routes, w_gate, w_up, w_down),
    )
    summed = call(sum_experts, shape(Z, 8, B), (swap(mixture, PLANE_AXES), ids))
    layer_out = call(finish_layer, shape(8, B), (swap(summed, "z"), mid_part))
    return context, layer_out.T


def solution(mesh):
    fine = Mesh(np.asarray(mesh.devices).reshape(X, Z, 2, 4), ALL_AXES)
    columns, rows = P(None, ALL_AXES), P(ALL_AXES, None)
    cache = P(None, ALL_AXES, None)
    placed = (
        columns,
        cache,
        cache,
        P(),
        columns,
        rows,
        P(),
        P(),
        P(),
        rows,
        rows,
        rows,
    )
    return jax.shard_map(
        shards,
        mesh=fine,
        in_specs=placed,
        out_specs=(columns, columns),
        check_vma=False,
    )
```

time: 158 us -> 145 us (0.918)
  blocking collectives: 103 us -> 136 us
  waiting for transfers between devices: 20.2 us -> 0 us
  starting transfers between devices: 16.6 us -> 0 us
  local copies, waits for them, and re-layouts: 6.58 us -> 0.69 us
  Pallas kernels: 10 us -> 7.12 us
    all_to_all x6 -> x8, blocking collectives: 103 us -> 136 us  [swap(): return lax.all_to_all(blocks, axes, 0, 0, tiled=True)]
    all_to_all x2 -> x0, waiting for transfers between devices: 20.2 us -> none  [swap(): return lax.all_to_all(blocks, axes, 0, 0, tiled=True)]
    all_to_all x2 -> x0, starting transfers between devices: 16.6 us -> none  [swap(): return lax.all_to_all(blocks, axes, 0, 0, tiled=True)]
    unnamed x26 -> x20, local copies, waits for them, and re-layouts: 6.49 us -> 0.69 us
    pallas_call x9, Pallas kernels: 10 us -> 7.12 us  [call(): pl.pallas_call(body, out_shape=outs, in_specs=[vmem] * len(arrays) + [rem...]
  transfers between devices with their start and end apart: 2 -> 0, of which waited for: 2 -> 0; matrix products, arithmetic and copies ran while one was open for 0% -> 0% of each run, Pallas kernels for 0% -> 0%
where the time goes in v3:
time: 145 us
  blocking collectives  136 us (94%)
  Pallas kernels  7.12 us (5%)
    all_to_all x8, blocking collectives, swap(): return lax.all_to_all(blocks, axes, 0, 0, tiled=True)  136 us
    pallas_call x9, Pallas kernels, call(): pl.pallas_call(body, out_shape=outs, in_specs=[vmem] * len(arrays) + [rem...  7.12 us

profile of v3, /device:TPU:1, one launch (start us, length us, event | category | flops | bytes accessed | tf_op | source)
XLA Modules:
  0.0 144.5 jit_solution(633290320043456615)
XLA Ops:
  0.6 1.7 %shard_map.131 = bf16[16,40,128]{2,1,0:T(8,128)(2,1)} custom-call(bf16[16,16]{1,0:T(8,128)(2,1)} %query.1, bf16[16,4096]{1,0:T(8,128)(2,1)} %out_proj.1), custom_call_target="tpu_custom_call" | custom-call | tf_op jit(solution)/shard_map/pallas_call | solution.py:288
  2.3 0.0 copy-start.4
  2.4 28.1 %all_to_all.40.arrived.dealt = bf16[16,40,128]{2,1,0:T(8,128)(2,1)S(1)} all-to-all(bf16[16,40,128]{2,1,0:T(8,128)(2,1)} %shard_map.131), channel_id=1, replica_groups=mesh['x'=4,'z'=16,'c'=2,'y'=4] {'z'}, dimensions={0} | all-to-all | bytes 327680 | tf_op jit(solution)/shard_map/all_to_all | solution.py:299
  30.5 0.0 copy-start.3
  30.5 0.2 shard_map.132
  30.7 0.0 copy-start.8
  30.7 20.1 %all_to_all.41.gathered = bf16[32,32,128]{2,1,0:T(8,128)(2,1)S(1)} all-to-all(bf16[32,32,128]{2,1,0:T(8,128)(2,1)S(1)} %shard_map.132), channel_id=1, replica_groups=mesh['x'=4,'z'=16,'c'=2,'y'=4] {'x','c','y'}, dimensions={0} | all-to-all | bytes 524288 | tf_op jit(solution)/shard_map/all_to_all | solution.py:299
  50.7 0.0 copy-start.9
  50.7 0.0 copy-done.4
  50.7 0.0 copy-done.3
  50.7 0.0 copy-done.8
  50.8 0.6 copy-done.9
  51.4 0.0 copy-start.2
  51.4 1.4 shard_map.133
  52.8 0.0 copy-start.1
  52.8 13.5 %all_to_all.42.arrived = bf16[32,40,128]{2,1,0:T(8,128)(2,1)S(1)} all-to-all(bf16[32,40,128]{2,1,0:T(8,128)(2,1)S(1)} %shard_map.133), channel_id=1, replica_groups=mesh['x'=4,'z'=16,'c'=2,'y'=4] {'x','c','y'}, dimensions={0} | all-to-all | bytes 655360 | tf_op jit(solution)/shard_map/all_to_all | solution.py:299
  66.3 0.0 copy-start
  66.3 0.3 shard_map.134
  66.7 16.0 %all_to_all.43.arrived = bf16[16,40,128]{2,1,0:T(8,128)(2,1)S(1)} all-to-all(bf16[16,40,128]{2,1,0:T(8,128)(2,1)S(1)} %get-tuple-element.8), channel_id=1, replica_groups=mesh['x'=4,'z'=16,'c'=2,'y'=4] {'z'}, dimensions={0} | all-to-all | bytes 327680 | tf_op jit(solution)/shard_map/all_to_all | solution.py:299
  82.7 0.8 shard_map.135
  83.5 0.0 copy-start.5
  83.5 16.3 %all_to_all.44.arrived = bf16[32,16,256]{2,1,0:T(8,128)(2,1)S(1)} all-to-all(bf16[32,16,256]{2,1,0:T(8,128)(2,1)S(1)} %get-tuple-element.10), channel_id=1, replica_groups=mesh['x'=4,'z'=16,'c'=2,'y'=4] {'x','c','y'}, dimensions={0} | all-to-all | bytes 524288 | tf_op jit(solution)/shard_map/all_to_all | solution.py:299
  99.8 0.0 copy-done.5
  99.8 0.3 shard_map.136
  100.1 0.0 copy-start.6
  100.1 0.0 copy-start.7
  100.1 15.3 %all_to_all.45.arrived = bf16[16,8,128]{2,1,0:T(8,128)(2,1)S(1)} all-to-all(bf16[16,8,128]{2,1,0:T(8,128)(2,1)S(1)} %get-tuple-element.12), channel_id=1, replica_groups=mesh['x'=4,'z'=16,'c'=2,'y'=4] {'z'}, dimensions={0} | all-to-all | bytes 65536 | tf_op jit(solution)/shard_map/all_to_all | solution.py:299
  115.4 0.0 copy-done.2
  115.4 0.0 copy-done.1
  115.4 0.0 copy-done
  115.4 0.0 copy-done.6
  115.4 0.0 copy-done.7
  115.4 1.5 %shard_map.137 = bf16[32,8,128]{2,1,0:T(8,128)(2,1)S(1)} custom-call(bf16[16,8,128]{2,1,0:T(8,128)(2,1)S(1)} %all_to_all.45.arrived, bf16[32,128]{1,0:T(8,128)(2,1)S(1)} %bitcast.8, s32[8,16]{1,0:T(8,128)S(1)} %bitcast.6, f32[8,16]{1,0:T(8,128)S(1)} %bitcast.9, bf16[128,4096]{1,0:T(8,128)(2,1)S(1)} %copy-done, bf16[128,4096]{1,0:T(8,128)(2,1)S(1)} %copy-done.1, ...), custom_call_target="tpu_custom_call" | custom-call | tf_op jit(solution)/shard_map/pallas_call | solution.py:288
  116.9 12.6 %all_to_all.46.arrived = bf16[32,8,128]{2,1,0:T(8,128)(2,1)S(1)} all-to-all(bf16[32,8,128]{2,1,0:T(8,128)(2,1)S(1)} %shard_map.137), channel_id=1, replica_groups=mesh['x'=4,'z'=16,'c'=2,'y'=4] {'x','c','y'}, dimensions={0} | all-to-all | bytes 131072 | tf_op jit(solution)/shard_map/all_to_all | solution.py:299
  129.5 0.3 shard_map.138
  129.9 14.1 %all_to_all.47.arrived = bf16[16,8,16]{2,1,0:T(8,128)(2,1)S(1)} all-to-all(bf16[16,8,16]{2,1,0:T(8,128)(2,1)S(1)} %shard_map.138), channel_id=1, replica_groups=mesh['x'=4,'z'=16,'c'=2,'y'=4] {'z'}, dimensions={0} | all-to-all | bytes 8192 | tf_op jit(solution)/shard_map/all_to_all | solution.py:299
  143.9 0.6 shard_map.139
Async XLA Ops:
  2.3 48.4 %copy-start.4 = (bf16[16,32,512]{2,1,0:T(8,128)(2,1)S(1)}, bf16[16,32,512]{2,1,0:T(8,128)(2,1)}, u32[]{:S(2)}) copy-start(bf16[16,32,512]{2,1,0:T(8,128)(2,1)} %values.1) | copy-start | bytes 1572868
  30.5 20.3 %copy-start.3 = (bf16[16,32,512]{2,1,0:T(8,128)(2,1)S(1)}, bf16[16,32,512]{2,1,0:T(8,128)(2,1)}, u32[]{:S(2)}) copy-start(bf16[16,32,512]{2,1,0:T(8,128)(2,1)} %keys.1) | copy-start | bytes 1572868
  30.7 20.1 %copy-start.8 = (bf16[16,8]{0,1:T(8,128)(2,1)S(1)}, bf16[16,8]{0,1:T(8,128)(2,1)}, u32[]{:S(2)}) copy-start(bf16[16,8]{0,1:T(8,128)(2,1)} %param.16) | copy-start | bytes 772
  50.7 0.7 copy-start.9
  51.4 64.0 %copy-start.2 = (bf16[128,4096]{1,0:T(8,128)(2,1)S(1)}, bf16[128,4096]{1,0:T(8,128)(2,1)}, u32[]{:S(2)}) copy-start(bf16[128,4096]{1,0:T(8,128)(2,1)} %w_down.1) | copy-start | bytes 3145732
  52.8 62.6 %copy-start.1 = (bf16[128,4096]{1,0:T(8,128)(2,1)S(1)}, bf16[128,4096]{1,0:T(8,128)(2,1)}, u32[]{:S(2)}) copy-start(bf16[128,4096]{1,0:T(8,128)(2,1)} %w_up.1) | copy-start | bytes 3145732
  66.3 49.1 %copy-start = (bf16[128,4096]{1,0:T(8,128)(2,1)S(1)}, bf16[128,4096]{1,0:T(8,128)(2,1)}, u32[]{:S(2)}) copy-start(bf16[128,4096]{1,0:T(8,128)(2,1)} %w_gate.1) | copy-start | bytes 3145732
  83.5 16.3 %copy-start.5 = (s32[16,8]{0,1:T(8,128)S(1)}, s32[16,8]{0,1:T(8,128)}, u32[]{:S(2)}) copy-start(s32[16,8]{0,1:T(8,128)} %param.19) | copy-start | bytes 1540
  100.1 15.3 %copy-start.6 = (bf16[4096]{0:T(1024)(128)(2,1)S(1)}, bf16[4096]{0:T(1024)(128)(2,1)}, u32[]{:S(2)}) copy-start(bf16[4096]{0:T(1024)(128)(2,1)} %param.18) | copy-start | bytes 24580
  100.1 15.3 %copy-start.7 = (f32[16,8]{0,1:T(8,128)S(1)}, f32[16,8]{0,1:T(8,128)}, u32[]{:S(2)}) copy-start(f32[16,8]{0,1:T(8,128)} %param.20) | copy-start | bytes 1540

commit v4 on v3

--- a/solution.py
+++ b/solution.py
@@ -50,10 +50,10 @@
     return x, z, lax.axis_index("c") * 4 + lax.axis_index("y")
 
 
-def deal_out(query, out_proj, out, held_query, held, sems):
+def pack_query(query, lengths, out, limits, held_query, held_lengths, sems):
     copies = [
         pltpu.make_async_copy(query, held_query, sems.at[0]),
-        pltpu.make_async_copy(out_proj, held, sems.at[1]),
+        pltpu.make_async_copy(lengths, held_lengths, sems.at[1]),
     ]
     for copy in copies:
         copy.start()
@@ -63,47 +63,62 @@
     for i in range(2):
         put = (iota((16, 128), 0) + i * 16 == iota((16, 128), 1)).astype(BF)
         parts.append(dot(own, put, ((1,), (0,)))[i * 8 : (i + 1) * 8])
-    wide = parts[0] + parts[1]
+    wide = (parts[0] + parts[1]).astype(BF)
+    for z in range(Z):
+        out[z] = wide
     copies[1].wait()
-    for v in range(Z // 2):
-        tiles = [
-            held[:, x * 1024 + v * 128 : x * 1024 + (v + 1) * 128].astype(F32) for x in range(X)
-        ]
-        for high in range(2):
-            pieces = [halves(tiles[0], tiles[1], high), halves(tiles[2], tiles[3], high), wide]
-            out[2 * v + high] = jnp.concatenate(pieces, axis=0).astype(BF)
+    rows = [jnp.full((1, 128), held_lengths[b], jnp.int32) for b in range(B)]
+    limits[...] = jnp.concatenate(rows, axis=0)
 
 
 def spread_query(arrived, out):
-    rows = arrived[:, 32:40, :].astype(F32).reshape(128, 128).astype(BF)
+    rows = arrived[...].astype(F32).reshape(128, 128).astype(BF)
     turned = dot(rows, eye(128), ((0,), (0,)))[:32].astype(BF)
     for k in range(PLANE):
         out[k] = turned
 
 
-def attend(gathered, keys, values, hidden, lengths, out, held_lengths, sem):
-    copy = pltpu.make_async_copy(lengths, held_lengths, sem)
-    copy.start()
+def attend(
+    gathered, keys, values, hidden, limits, out, held_keys, held_values, held_hidden, held_limits, sems
+):
+    copies = [
+        pltpu.make_async_copy(limits, held_limits, sems.at[0]),
+        pltpu.make_async_copy(hidden, held_hidden, sems.at[1]),
+    ]
+    for n, (source, target) in enumerate(((keys, held_keys), (values, held_values))):
+        for i in range(2):
+            part = pl.ds(i * 8, 8)
+            copies.append(
+                pltpu.make_async_copy(source.at[part], target.at[part], sems.at[2 + 2 * n + i])
+            )
+    for copy in copies:
+        copy.start()
     x, z, cy = coordinates()
     device = (x * Z + z) * CY + cy
     lane_j = iota((SPAN, 128), 1) % 8
     position = device * SPAN + iota((SPAN, 128), 0)
+    copies[0].wait()
+    copies[1].wait()
     spot = (iota((B, 128), 0) == iota((B, 128), 1) % B).astype(BF)
-    repeated = dot(hidden[...], spot, ((1,), (0,)))
+    repeated = dot(held_hidden[...], spot, ((1,), (0,)))
     own = jnp.where(iota((8, 128), 0) == iota((8, 128), 1) // B, repeated, 0.0)
     own = jnp.sum(own, axis=0, keepdims=True)
     zero = jnp.zeros((1, 128), F32)
-    copy.wait()
+    limit = held_limits[...]
     valids = []
     for i in range(2):
-        rows = [(lane_j == j) & (position < held_lengths[i * 8 + j]) for j in range(8)]
+        rows = [
+            (lane_j == j) & (position < limit[i * 8 + j : i * 8 + j + 1]) for j in range(8)
+        ]
         valids.append(jnp.concatenate([r.astype(F32) for r in rows], axis=0) > 0.5)
+    for copy in copies[2:]:
+        copy.wait()
     for g in range(X):
         parts, tops, highs, lows = [], [], [], []
         for i in range(2):
             query = gathered[g * CY : (g + 1) * CY, i * 16 : (i + 1) * 16, :].reshape(HD, 128)
-            k = keys[i * 8 : (i + 1) * 8, :, g * HD : (g + 1) * HD].reshape(8 * SPAN, HD)
-            v = values[i * 8 : (i + 1) * 8, :, g * HD : (g + 1) * HD].reshape(8 * SPAN, HD)
+            k = held_keys[i * 8 : (i + 1) * 8, :, g * HD : (g + 1) * HD].reshape(8 * SPAN, HD)
+            v = held_values[i * 8 : (i + 1) * 8, :, g * HD : (g + 1) * HD].reshape(8 * SPAN, HD)
             scores = dot(k, query, ((1,), (0,))) * (1.0 / math.sqrt(HD))
             scores = jnp.where(valids[i], scores, FLOOR)
             top = jnp.max(scores, axis=0, keepdims=True).astype(BF).astype(F32)
@@ -153,12 +168,20 @@
         hidden_cols[:, t * 128 : (t + 1) * 128] = jnp.sum(by_lane, axis=0)
 
 
-def finish_context(arrived, dealt, context, out):
+def finish_context(arrived, out_proj, context, out, weights, sems):
     z = lax.axis_index("z")
-    weights = jnp.concatenate(
-        [dealt[:, t * 16 : (t + 1) * 16, :].reshape(Z * 16, 128) for t in range(2)], axis=1
-    )
-    contexts, terms = [], []
+    copies = []
+    for x in range(X):
+        start = pl.multiple_of(x * 1024 + z // 2 * 128, 128)
+        copies.append(
+            pltpu.make_async_copy(
+                out_proj.at[:, pl.ds(start, 128)],
+                weights.at[:, x * 128 : (x + 1) * 128],
+                sems.at[x],
+            )
+        )
+        copies[x].start()
+    contexts, blocks = [], []
     for i in range(2):
         mixed, _, mass = merge(arrived, i)
         done = (mixed / mass).astype(BF)
@@ -167,11 +190,22 @@
         tile = (iota((16, 256), 0) == iota((16, 256), 1) % 16).astype(BF)
         tiled = dot(done, tile, ((0,), (0,)))
         block = iota((128, 256), 0) // 8 == iota((128, 256), 1) // 16
-        tiled = jnp.where(block, tiled, 0.0).astype(BF)
-        term = dot(tiled, weights, ((1,), (0,)))
-        terms.append(jnp.sum(term.reshape(Z, 8, COLS), axis=0))
+        blocks.append(jnp.where(block, tiled, 0.0).astype(BF))
     context[...] = jnp.concatenate(contexts, axis=0).astype(BF)
-    term = jnp.concatenate(terms, axis=0).astype(BF)
+    for copy in copies:
+        copy.wait()
+    terms = []
+    for i in range(2):
+        term = dot(blocks[i], weights[...], ((1,), (0,)))
+        terms.append(jnp.sum(term.reshape(Z, 8, 512), axis=0))
+    term = jnp.concatenate(terms, axis=0)
+    tiles = [term[:, x * 128 : (x + 1) * 128] for x in range(X)]
+    odd = (iota((B, 128), 0) * 0 + z) % 2 == 1
+    parts = [
+        jnp.where(odd, halves(first, second, 1), halves(first, second, 0))
+        for first, second in (tiles[:2], tiles[2:])
+    ]
+    term = jnp.concatenate(parts, axis=1).astype(BF)
     for k in range(PLANE):
         out[k] = term
 
@@ -225,7 +259,18 @@
     return tiles
 
 
-def experts(arrived, gain, expert_ids, route_weights, w_gate, w_up, w_down, out):
+def experts(
+    arrived, gain, expert_ids, route_weights, w_gate, w_up, w_down, out, held, sems
+):
+    copies = []
+    for n, source in enumerate((w_gate, w_up, w_down)):
+        for h in range(2):
+            part = pl.ds(h * 64, 64)
+            copies.append(
+                pltpu.make_async_copy(source.at[part], held.at[n, part], sems.at[2 * n + h])
+            )
+    for copy in copies:
+        copy.start()
     x, z, _ = coordinates()
     expert = x * Z + z
     ids = expert_ids[...]
@@ -255,10 +300,17 @@
         far = dot(picked, weights[:, D // 2 :], ((1,), (1,)))
         return near + jnp.concatenate([far[4:], far[:4]], axis=0)
 
-    gate = project(w_gate)
-    upward = project(w_up)
+    halves_of = [copies[2 * n : 2 * n + 2] for n in range(3)]
+    for copy in halves_of[0]:
+        copy.wait()
+    gate = project(held.at[0])
+    for copy in halves_of[1]:
+        copy.wait()
+    upward = project(held.at[1])
     hidden_units = (gate / (1.0 + jnp.exp(-gate)) * upward).astype(BF)
-    weighted = dot(hidden_units, w_down[...], ((1,), (0,))) * coefficient
+    for copy in halves_of[2]:
+        copy.wait()
+    weighted = dot(hidden_units, held[2], ((1,), (0,))) * coefficient
     for group in range(X):
         start = group * 1024
         tiles = [weighted[:, start + v * 128 : start + (v + 1) * 128] for v in range(8)]
@@ -319,24 +371,24 @@
     def shape(*dims, dtype=BF):
         return jax.ShapeDtypeStruct(dims, dtype)
 
-    dealt = swap(
-        call(
-            deal_out,
-            shape(Z, 40, 128),
-            (),
-            (query, out_proj),
-            (vmem((B, 16), BF), vmem((16, D), BF), dma((2,))),
-            62,
-        ),
-        "z",
-    )
-    gathered = swap(call(spread_query, shape(PLANE, 32, 128), (dealt,)), PLANE_AXES)
+    rows = lax.all_gather(out_proj, "z", axis=0, tiled=True)
+    packed, limits = call(
+        pack_query,
+        [shape(Z, 8, 128), shape(B, 128, dtype=jnp.int32)],
+        (),
+        (query, lengths),
+        (vmem((B, 16), BF), pltpu.SMEM((B,), jnp.int32), dma((2,))),
+        62,
+    )
+    spread = call(spread_query, shape(PLANE, 32, 128), (swap(packed, "z"),))
+    cache = vmem((B, SPAN, 512), BF)
     partial = call(
         attend,
         shape(PLANE, 40, 128),
-        (gathered, key_cache, value_cache, hidden_in.T),
-        (lengths,),
-        (pltpu.SMEM((B,), jnp.int32), dma),
+        (swap(spread, PLANE_AXES),),
+        (key_cache, value_cache, hidden_in.T, limits),
+        (cache, cache, vmem((8, B), BF), vmem((B, 128), jnp.int32), dma((6,))),
+        62,
     )
     merged, hidden_cols = call(
         merge_plane,
@@ -346,7 +398,10 @@
     context, term = call(
         finish_context,
         [shape(B, 16), shape(PLANE, B, COLS)],
-        (swap(merged, "z"), dealt),
+        (swap(merged, "z"),),
+        (rows,),
+        (vmem((Z * 16, 512), BF), dma((X,))),
+        62,
     )
     picked, mid_part = call(
         make_mid,
@@ -356,7 +411,10 @@
     mixture = call(
         experts,
         shape(PLANE, 8, 128),
-        (swap(picked, "z"), norm_gain.reshape(PLANE, 128), ids, routes, w_gate, w_up, w_down),
+        (swap(picked, "z"), norm_gain.reshape(PLANE, 128), ids, routes),
+        (w_gate, w_up, w_down),
+        (vmem((3, 128, D), BF), dma((6,))),
+        62,
     )
     summed = call(sum_experts, shape(Z, 8, B), (swap(mixture, PLANE_AXES), ids))
     layer_out = call(finish_layer, shape(8, B), (swap(summed, "z"), mid_part))

time: 145 us -> 170 us (1.17)
  between operations: 0.75 us -> 14.1 us
  Pallas kernels: 7.12 us -> 14.1 us
  blocking collectives: 136 us -> 140 us
    pallas_call x9, Pallas kernels: 7.12 us -> 14.1 us  [call(): pl.pallas_call(body, out_shape=outs, in_specs=[vmem] * len(arrays) + [rem...]
    all_to_all x8, blocking collectives: 136 us -> 140 us  [swap(): return lax.all_to_all(blocks, axes, 0, 0, tiled=True)]
  transfers between devices with their start and end apart: 0 -> 1, of which waited for: 0 -> 0; matrix products, arithmetic and copies ran while one was open for 0% -> 0% of each run, Pallas kernels for 0% -> 3%
where the time goes in v4:
time: 170 us; the launch traced here: 169 us
  blocking collectives  140 us (82%)
  Pallas kernels  14.1 us (8%)
  between operations  14.1 us (8%)
    all_to_all x8, blocking collectives, swap(): return lax.all_to_all(blocks, axes, 0, 0, tiled=True)  140 us
    pallas_call x9, Pallas kernels, call(): pl.pallas_call(body, out_shape=outs, in_specs=[vmem] * len(arrays) + [rem...  14.1 us
  transfers between devices with their start and end apart: 1, of which 0 were waited for; matrix products, arithmetic and copies ran while one was open for 0% of the time, Pallas kernels for 3%

profile of v4, /device:TPU:1, one launch (start us, length us, event | category | flops | bytes accessed | tf_op | source)
XLA Modules:
  0.0 169.3 jit_solution(11077293290612183867)
XLA Ops:
  7.2 0.0 all-gather.2.cloned.1.call-start
  7.2 0.7 all-gather.2.cloned.1.call-update
  7.9 1.5 shard_map.131
  9.4 27.2 %all_to_all.40.arrived = bf16[16,8,128]{2,1,0:T(8,128)(2,1)S(1)} all-to-all(bf16[16,8,128]{2,1,0:T(8,128)(2,1)} %get-tuple-element.10), channel_id=1, replica_groups=mesh['x'=4,'z'=16,'c'=2,'y'=4] {'z'}, dimensions={0} | all-to-all | bytes 65536 | tf_op jit(solution)/shard_map/all_to_all | solution.py:351
  36.6 0.2 shard_map.132
  36.8 18.0 %all_to_all.41.gathered = bf16[32,32,128]{2,1,0:T(8,128)(2,1)} all-to-all(bf16[32,32,128]{2,1,0:T(8,128)(2,1)S(1)} %shard_map.132), channel_id=1, replica_groups=mesh['x'=4,'z'=16,'c'=2,'y'=4] {'x','c','y'}, dimensions={0} | all-to-all | bytes 524288 | tf_op jit(solution)/shard_map/all_to_all | solution.py:351
  54.8 3.8 %shard_map.133 = bf16[32,40,128]{2,1,0:T(8,128)(2,1)} custom-call(bf16[32,32,128]{2,1,0:T(8,128)(2,1)} %all_to_all.41.gathered, bf16[16,32,512]{2,1,0:T(8,128)(2,1)} %keys.1, bf16[16,32,512]{2,1,0:T(8,128)(2,1)} %values.1, bf16[8,16]{1,0:T(8,128)(2,1)} %bitcast.10, s32[16,128]{1,0:T(8,128)} %get-tuple-element.11.limits), custom_call_target="tpu_custom_call" | custom-call | tf_op jit(solution)/shard_map/pallas_call | solution.py:340
  58.6 0.0 copy-start
  58.6 13.7 %all_to_all.42.arrived = bf16[32,40,128]{2,1,0:T(8,128)(2,1)S(1)} all-to-all(bf16[32,40,128]{2,1,0:T(8,128)(2,1)} %shard_map.133), channel_id=1, replica_groups=mesh['x'=4,'z'=16,'c'=2,'y'=4] {'x','c','y'}, dimensions={0} | all-to-all | bytes 655360 | tf_op jit(solution)/shard_map/all_to_all | solution.py:351
  72.3 0.3 shard_map.134
  72.6 16.9 %all_to_all.43.arrived = bf16[16,40,128]{2,1,0:T(8,128)(2,1)} all-to-all(bf16[16,40,128]{2,1,0:T(8,128)(2,1)S(1)} %get-tuple-element.12), channel_id=1, replica_groups=mesh['x'=4,'z'=16,'c'=2,'y'=4] {'z'}, dimensions={0} | all-to-all | bytes 327680 | tf_op jit(solution)/shard_map/all_to_all | solution.py:351
  89.5 0.0 all-gather.2.cloned.1.call-done.out_proj
  89.5 3.0 %shard_map.135 = (bf16[16,16]{1,0:T(8,128)(2,1)}, bf16[32,16,256]{2,1,0:T(8,128)(2,1)}) custom-call(bf16[16,40,128]{2,1,0:T(8,128)(2,1)} %all_to_all.43.arrived, bf16[256,4096]{1,0:T(8,128)(2,1)} %all-gather.2.cloned.1.call-done.out_proj), custom_call_target="tpu_custom_call" | custom-call | tf_op jit(solution)/shard_map/pallas_call | solution.py:340
  92.5 0.0 copy-start.1
  92.5 19.0 %all_to_all.44.arrived = bf16[32,16,256]{2,1,0:T(8,128)(2,1)S(1)} all-to-all(bf16[32,16,256]{2,1,0:T(8,128)(2,1)} %get-tuple-element.14), channel_id=1, replica_groups=mesh['x'=4,'z'=16,'c'=2,'y'=4] {'x','c','y'}, dimensions={0} | all-to-all | bytes 524288 | tf_op jit(solution)/shard_map/all_to_all | solution.py:351
  111.5 0.0 copy-done
  111.5 0.3 shard_map.136
  111.8 18.7 %all_to_all.45.arrived = bf16[16,8,128]{2,1,0:T(8,128)(2,1)} all-to-all(bf16[16,8,128]{2,1,0:T(8,128)(2,1)S(1)} %get-tuple-element.16), channel_id=1, replica_groups=mesh['x'=4,'z'=16,'c'=2,'y'=4] {'z'}, dimensions={0} | all-to-all | bytes 65536 | tf_op jit(solution)/shard_map/all_to_all | solution.py:351
  130.5 4.1 %shard_map.137 = bf16[32,8,128]{2,1,0:T(8,128)(2,1)} custom-call(bf16[16,8,128]{2,1,0:T(8,128)(2,1)} %all_to_all.45.arrived, bf16[32,128]{1,0:T(8,128)(2,1)} %bitcast.8, s32[8,16]{1,0:T(8,128)} %bitcast.5, f32[8,16]{1,0:T(8,128)} %bitcast.9, bf16[128,4096]{1,0:T(8,128)(2,1)} %w_gate.1, bf16[128,4096]{1,0:T(8,128)(2,1)} %w_up.1, bf16[128,4096]{1,0:T(8,128)(2,1)} %w_down.1), custom_call_target="tpu_custom_call" | custom-call | tf_op jit(solution)/shard_map/pallas_call | solution.py:340
  134.6 12.8 %all_to_all.46.arrived = bf16[32,8,128]{2,1,0:T(8,128)(2,1)S(1)} all-to-all(bf16[32,8,128]{2,1,0:T(8,128)(2,1)} %shard_map.137), channel_id=1, replica_groups=mesh['x'=4,'z'=16,'c'=2,'y'=4] {'x','c','y'}, dimensions={0} | all-to-all | bytes 131072 | tf_op jit(solution)/shard_map/all_to_all | solution.py:351
  147.5 0.0 copy-done.1
  147.5 0.3 shard_map.138
  147.8 14.1 %all_to_all.47.arrived = bf16[16,8,16]{2,1,0:T(8,128)(2,1)S(1)} all-to-all(bf16[16,8,16]{2,1,0:T(8,128)(2,1)S(1)} %shard_map.138), channel_id=1, replica_groups=mesh['x'=4,'z'=16,'c'=2,'y'=4] {'z'}, dimensions={0} | all-to-all | bytes 8192 | tf_op jit(solution)/shard_map/all_to_all | solution.py:351
  161.9 0.6 shard_map.139
Async XLA Ops:
  7.2 82.3 %all-gather.2.cloned.1.call-start = ((), (), s32[]{:S(2)}) async-start(), calls=%async_computation.8 | async-start | bytes 2228224 | tf_op jit(solution)/shard_map/all_gather | solution.py:374
  58.6 52.9 %copy-start = (s32[16,8]{0,1:T(8,128)S(1)}, s32[16,8]{0,1:T(8,128)}, u32[]{:S(2)}) copy-start(s32[16,8]{0,1:T(8,128)} %param.19) | copy-start | bytes 1540
  92.5 55.0 %copy-start.1 = (s32[16,8]{0,1:T(8,128)S(1)}, s32[16,8]{0,1:T(8,128)}, u32[]{:S(2)}) copy-start(s32[16,8]{0,1:T(8,128)} %param.19) | copy-start | bytes 1540
Sparse Core Ops, SparseCore 0:
  10.1 69.7 all-gather.1

commit v5 on v3

--- a/solution.py
+++ b/solution.py
@@ -63,40 +63,45 @@
     for i in range(2):
         put = (iota((16, 128), 0) + i * 16 == iota((16, 128), 1)).astype(BF)
         parts.append(dot(own, put, ((1,), (0,)))[i * 8 : (i + 1) * 8])
-    wide = parts[0] + parts[1]
+    wide = (parts[0] + parts[1]).astype(BF)
     copies[1].wait()
     for v in range(Z // 2):
         tiles = [
-            held[:, x * 1024 + v * 128 : x * 1024 + (v + 1) * 128].astype(F32) for x in range(X)
+            held[:, x * 1024 + v * 128 : x * 1024 + (v + 1) * 128] for x in range(X)
         ]
         for high in range(2):
             pieces = [halves(tiles[0], tiles[1], high), halves(tiles[2], tiles[3], high), wide]
-            out[2 * v + high] = jnp.concatenate(pieces, axis=0).astype(BF)
-
-
-def spread_query(arrived, out):
+            out[2 * v + high] = jnp.concatenate(pieces, axis=0)
+
+
+def spread_query(arrived, lengths, hidden, out, rows_out):
     rows = arrived[:, 32:40, :].astype(F32).reshape(128, 128).astype(BF)
     turned = dot(rows, eye(128), ((0,), (0,)))[:32].astype(BF)
     for k in range(PLANE):
         out[k] = turned
-
-
-def attend(gathered, keys, values, hidden, lengths, out, held_lengths, sem):
-    copy = pltpu.make_async_copy(lengths, held_lengths, sem)
-    copy.start()
+    own = iota((B, B), 0) == iota((B, B), 1)
+    column = jnp.sum(jnp.where(own, lengths[...].astype(F32), 0.0), axis=1, keepdims=True)
+    rows_out[0:B] = jnp.broadcast_to(column, (B, 128))
+    spot = (iota((B, 128), 0) == iota((B, 128), 1) % B).astype(BF)
+    repeated = dot(hidden[...], spot, ((1,), (0,)))
+    own = jnp.where(iota((8, 128), 0) == iota((8, 128), 1) // B, repeated, 0.0)
+    rows_out[B : B + 8] = jnp.broadcast_to(jnp.sum(own, axis=0, keepdims=True), (8, 128))
+
+
+def attend(gathered, keys, values, extra, out):
     x, z, cy = coordinates()
     device = (x * Z + z) * CY + cy
     lane_j = iota((SPAN, 128), 1) % 8
     position = device * SPAN + iota((SPAN, 128), 0)
-    spot = (iota((B, 128), 0) == iota((B, 128), 1) % B).astype(BF)
-    repeated = dot(hidden[...], spot, ((1,), (0,)))
-    own = jnp.where(iota((8, 128), 0) == iota((8, 128), 1) // B, repeated, 0.0)
-    own = jnp.sum(own, axis=0, keepdims=True)
+    own = extra[B : B + 1]
     zero = jnp.zeros((1, 128), F32)
-    copy.wait()
+    position = position.astype(F32)
+    limit = extra[0:B]
     valids = []
     for i in range(2):
-        rows = [(lane_j == j) & (position < held_lengths[i * 8 + j]) for j in range(8)]
+        rows = [
+            (lane_j == j) & (position < limit[i * 8 + j : i * 8 + j + 1]) for j in range(8)
+        ]
         valids.append(jnp.concatenate([r.astype(F32) for r in rows], axis=0) > 0.5)
     for g in range(X):
         parts, tops, highs, lows = [], [], [], []
@@ -330,13 +335,15 @@
         ),
         "z",
     )
-    gathered = swap(call(spread_query, shape(PLANE, 32, 128), (dealt,)), PLANE_AXES)
+    spread, extra = call(
+        spread_query,
+        [shape(PLANE, 32, 128), shape(B + 8, 128, dtype=F32)],
+        (dealt, lengths.reshape(1, B), hidden_in.T),
+    )
     partial = call(
         attend,
         shape(PLANE, 40, 128),
-        (gathered, key_cache, value_cache, hidden_in.T),
-        (lengths,),
-        (pltpu.SMEM((B,), jnp.int32), dma),
+        (swap(spread, PLANE_AXES), key_cache, value_cache, extra),
     )
     merged, hidden_cols = call(
         merge_plane,

time: 145 us -> 144 us (level)
  no operation moved by 1% of the time
where the time goes in v5:
time: 144 us; the launch traced here: 143 us
  blocking collectives  136 us (94%)
  Pallas kernels  6.62 us (5%)
    all_to_all x8, blocking collectives, swap(): return lax.all_to_all(blocks, axes, 0, 0, tiled=True)  136 us
    pallas_call x9, Pallas kernels, call(): pl.pallas_call(body, out_shape=outs, in_specs=[vmem] * len(arrays) + [rem...  6.62 us

profile of v5, /device:TPU:1, one launch (start us, length us, event | category | flops | bytes accessed | tf_op | source)
XLA Modules:
  0.0 143.4 jit_solution(6033164495662981024)
XLA Ops:
  0.6 0.0 copy-start.8
  0.6 0.0 copy-start.9
  0.7 0.0 copy-start.4
  0.7 1.8 %shard_map.131 = bf16[16,40,128]{2,1,0:T(8,128)(2,1)} custom-call(bf16[16,16]{1,0:T(8,128)(2,1)} %query.1, bf16[16,4096]{1,0:T(8,128)(2,1)} %out_proj.1), custom_call_target="tpu_custom_call" | custom-call | tf_op jit(solution)/shard_map/pallas_call | solution.py:293
  2.4 0.0 copy-start.3
  2.4 28.1 %all_to_all.40.arrived.dealt = bf16[16,40,128]{2,1,0:T(8,128)(2,1)S(1)} all-to-all(bf16[16,40,128]{2,1,0:T(8,128)(2,1)} %shard_map.131), channel_id=1, replica_groups=mesh['x'=4,'z'=16,'c'=2,'y'=4] {'z'}, dimensions={0} | all-to-all | bytes 327680 | tf_op jit(solution)/shard_map/all_to_all | solution.py:304
  30.6 0.0 copy-done.8
  30.6 0.0 copy-done.9
  30.6 0.2 shard_map.132
  30.8 20.1 %all_to_all.41.gathered = bf16[32,32,128]{2,1,0:T(8,128)(2,1)S(1)} all-to-all(bf16[32,32,128]{2,1,0:T(8,128)(2,1)S(1)} %get-tuple-element.10), channel_id=1, replica_groups=mesh['x'=4,'z'=16,'c'=2,'y'=4] {'x','c','y'}, dimensions={0} | all-to-all | bytes 524288 | tf_op jit(solution)/shard_map/all_to_all | solution.py:304
  50.8 0.0 copy-done.4
  50.8 0.0 copy-done.3
  50.8 0.0 copy-start.2
  50.8 0.8 shard_map.133
  51.7 0.0 copy-start.1
  51.7 13.5 %all_to_all.42.arrived = bf16[32,40,128]{2,1,0:T(8,128)(2,1)S(1)} all-to-all(bf16[32,40,128]{2,1,0:T(8,128)(2,1)S(1)} %shard_map.133), channel_id=1, replica_groups=mesh['x'=4,'z'=16,'c'=2,'y'=4] {'x','c','y'}, dimensions={0} | all-to-all | bytes 655360 | tf_op jit(solution)/shard_map/all_to_all | solution.py:304
  65.2 0.0 copy-start
  65.2 0.3 shard_map.134
  65.5 16.0 %all_to_all.43.arrived = bf16[16,40,128]{2,1,0:T(8,128)(2,1)S(1)} all-to-all(bf16[16,40,128]{2,1,0:T(8,128)(2,1)S(1)} %get-tuple-element.12), channel_id=1, replica_groups=mesh['x'=4,'z'=16,'c'=2,'y'=4] {'z'}, dimensions={0} | all-to-all | bytes 327680 | tf_op jit(solution)/shard_map/all_to_all | solution.py:304
  81.6 0.8 shard_map.135
  82.4 0.0 copy-start.5
  82.4 16.3 %all_to_all.44.arrived = bf16[32,16,256]{2,1,0:T(8,128)(2,1)S(1)} all-to-all(bf16[32,16,256]{2,1,0:T(8,128)(2,1)S(1)} %get-tuple-element.14), channel_id=1, replica_groups=mesh['x'=4,'z'=16,'c'=2,'y'=4] {'x','c','y'}, dimensions={0} | all-to-all | bytes 524288 | tf_op jit(solution)/shard_map/all_to_all | solution.py:304
  98.6 0.0 copy-done.5
  98.6 0.3 shard_map.136
  99.0 0.0 copy-start.6
  99.0 0.0 copy-start.7
  99.0 15.3 %all_to_all.45.arrived = bf16[16,8,128]{2,1,0:T(8,128)(2,1)S(1)} all-to-all(bf16[16,8,128]{2,1,0:T(8,128)(2,1)S(1)} %get-tuple-element.16), channel_id=1, replica_groups=mesh['x'=4,'z'=16,'c'=2,'y'=4] {'z'}, dimensions={0} | all-to-all | bytes 65536 | tf_op jit(solution)/shard_map/all_to_all | solution.py:304
  114.3 0.0 copy-done.2
  114.3 0.0 copy-done.1
  114.3 0.0 copy-done
  114.3 0.0 copy-done.6
  114.3 0.0 copy-done.7
  114.3 1.5 %shard_map.137 = bf16[32,8,128]{2,1,0:T(8,128)(2,1)S(1)} custom-call(bf16[16,8,128]{2,1,0:T(8,128)(2,1)S(1)} %all_to_all.45.arrived, bf16[32,128]{1,0:T(8,128)(2,1)S(1)} %bitcast.9, s32[8,16]{1,0:T(8,128)S(1)} %bitcast.7, f32[8,16]{1,0:T(8,128)S(1)} %bitcast.10, bf16[128,4096]{1,0:T(8,128)(2,1)S(1)} %copy-done, bf16[128,4096]{1,0:T(8,128)(2,1)S(1)} %copy-done.1, ...), custom_call_target="tpu_custom_call" | custom-call | tf_op jit(solution)/shard_map/pallas_call | solution.py:293
  115.8 12.6 %all_to_all.46.arrived = bf16[32,8,128]{2,1,0:T(8,128)(2,1)S(1)} all-to-all(bf16[32,8,128]{2,1,0:T(8,128)(2,1)S(1)} %shard_map.137), channel_id=1, replica_groups=mesh['x'=4,'z'=16,'c'=2,'y'=4] {'x','c','y'}, dimensions={0} | all-to-all | bytes 131072 | tf_op jit(solution)/shard_map/all_to_all | solution.py:304
  128.4 0.3 shard_map.138
  128.7 14.1 %all_to_all.47.arrived = bf16[16,8,16]{2,1,0:T(8,128)(2,1)S(1)} all-to-all(bf16[16,8,16]{2,1,0:T(8,128)(2,1)S(1)} %shard_map.138), channel_id=1, replica_groups=mesh['x'=4,'z'=16,'c'=2,'y'=4] {'z'}, dimensions={0} | all-to-all | bytes 8192 | tf_op jit(solution)/shard_map/all_to_all | solution.py:304
  142.8 0.6 shard_map.139
Async XLA Ops:
  0.6 29.9 %copy-start.8 = (bf16[16,8]{0,1:T(8,128)(2,1)S(1)}, bf16[16,8]{0,1:T(8,128)(2,1)}, u32[]{:S(2)}) copy-start(bf16[16,8]{0,1:T(8,128)(2,1)} %param.16) | copy-start | bytes 772
  0.6 29.9 %copy-start.9 = (s32[16]{0:T(128)S(1)}, s32[16]{0:T(128)}, u32[]{:S(2)}) copy-start(s32[16]{0:T(128)} %param.15) | copy-start | bytes 196
  0.7 50.2 %copy-start.4 = (bf16[16,32,512]{2,1,0:T(8,128)(2,1)S(1)}, bf16[16,32,512]{2,1,0:T(8,128)(2,1)}, u32[]{:S(2)}) copy-start(bf16[16,32,512]{2,1,0:T(8,128)(2,1)} %values.1) | copy-start | bytes 1572868
  2.4 48.4 %copy-start.3 = (bf16[16,32,512]{2,1,0:T(8,128)(2,1)S(1)}, bf16[16,32,512]{2,1,0:T(8,128)(2,1)}, u32[]{:S(2)}) copy-start(bf16[16,32,512]{2,1,0:T(8,128)(2,1)} %keys.1) | copy-start | bytes 1572868
  50.8 63.5 %copy-start.2 = (bf16[128,4096]{1,0:T(8,128)(2,1)S(1)}, bf16[128,4096]{1,0:T(8,128)(2,1)}, u32[]{:S(2)}) copy-start(bf16[128,4096]{1,0:T(8,128)(2,1)} %w_down.1) | copy-start | bytes 3145732
  51.7 62.6 %copy-start.1 = (bf16[128,4096]{1,0:T(8,128)(2,1)S(1)}, bf16[128,4096]{1,0:T(8,128)(2,1)}, u32[]{:S(2)}) copy-start(bf16[128,4096]{1,0:T(8,128)(2,1)} %w_up.1) | copy-start | bytes 3145732
  65.2 49.1 %copy-start = (bf16[128,4096]{1,0:T(8,128)(2,1)S(1)}, bf16[128,4096]{1,0:T(8,128)(2,1)}, u32[]{:S(2)}) copy-start(bf16[128,4096]{1,0:T(8,128)(2,1)} %w_gate.1) | copy-start | bytes 3145732
  82.4 16.3 %copy-start.5 = (s32[16,8]{0,1:T(8,128)S(1)}, s32[16,8]{0,1:T(8,128)}, u32[]{:S(2)}) copy-start(s32[16,8]{0,1:T(8,128)} %param.19) | copy-start | bytes 1540
  99.0 15.3 %copy-start.6 = (bf16[4096]{0:T(1024)(128)(2,1)S(1)}, bf16[4096]{0:T(1024)(128)(2,1)}, u32[]{:S(2)}) copy-start(bf16[4096]{0:T(1024)(128)(2,1)} %param.18) | copy-start | bytes 24580
  99.0 15.3 %copy-start.7 = (f32[16,8]{0,1:T(8,128)S(1)}, f32[16,8]{0,1:T(8,128)}, u32[]{:S(2)}) copy-start(f32[16,8]{0,1:T(8,128)} %param.20) | copy-start | bytes 1540

commit v6 on v5

--- a/solution.py
+++ b/solution.py
@@ -268,7 +268,7 @@
         start = group * 1024
         tiles = [weighted[:, start + v * 128 : start + (v + 1) * 128] for v in range(8)]
         for c, tile in enumerate(sort_columns(tiles)):
-            out[group * CY + c] = tile.astype(BF)
+            out[group * CY + c] = tile[:4].astype(BF)
 
 
 def sum_experts(arrived, expert_ids, out):
@@ -276,14 +276,22 @@
     parts = [
         jnp.sum(arrived[x * CY : (x + 1) * CY].astype(F32), axis=0) for x in range(X)
     ]
-    row = iota((8 * X, B), 0)
-    table = slots(expert_ids[...], row // 8 * Z + z, row % 8).astype(F32)
-    turned = dot(jnp.concatenate(parts, axis=0), table, ((0,), (0,)), EXACT)
-    out[...] = turned.reshape(Z, 8, B).astype(BF)
+    row = iota((4 * X, B), 0)
+    table = slots(expert_ids[...], row // 4 * Z + z, row % 4).astype(F32)
+    turned = dot(jnp.concatenate(parts, axis=0), table, ((0,), (0,)), EXACT).astype(BF)
+    spot = (iota((B, 128), 0) == iota((B, 128), 1) % B).astype(BF)
+    wide = dot(turned, spot, ((1,), (0,)))
+    wide = jnp.where(iota((128, 128), 0) % 8 == iota((128, 128), 1) // B, wide, 0.0)
+    rows = jnp.sum(wide.reshape(Z, 8, 128), axis=1, keepdims=True)
+    out[...] = rows.astype(BF)
 
 
 def finish_layer(arrived, mid_part, out):
-    out[...] = (mid_part[...] + jnp.sum(arrived[...].astype(F32), axis=0)).astype(BF)
+    total = jnp.sum(arrived[...].astype(F32), axis=0)
+    wide = jnp.where(iota((8, 128), 0) == iota((8, 128), 1) // B, total, 0.0)
+    fold = (iota((128, B), 0) % B == iota((128, B), 1)).astype(F32)
+    mixture = dot(wide, fold, ((1,), (0,)), EXACT)
+    out[...] = (mid_part[...] + mixture).astype(BF)
 
 
 def call(body, outs, arrays, far=(), scratch=(), limit=16):
@@ -362,10 +370,10 @@
     )
     mixture = call(
         experts,
-        shape(PLANE, 8, 128),
+        shape(PLANE, 4, 128),
         (swap(picked, "z"), norm_gain.reshape(PLANE, 128), ids, routes, w_gate, w_up, w_down),
     )
-    summed = call(sum_experts, shape(Z, 8, B), (swap(mixture, PLANE_AXES), ids))
+    summed = call(sum_experts, shape(Z, 1, 128), (swap(mixture, PLANE_AXES), ids))
     layer_out = call(finish_layer, shape(8, B), (swap(summed, "z"), mid_part))
     return context, layer_out.T
 

time: 144 us -> 144 us (level)
  no operation moved by 1% of the time
where the time goes in v6:
time: 144 us; the launch traced here: 143 us
  blocking collectives  136 us (94%)
  Pallas kernels  6.92 us (5%)
    all_to_all x8, blocking collectives, swap(): return lax.all_to_all(blocks, axes, 0, 0, tiled=True)  136 us
    pallas_call x9, Pallas kernels, call(): pl.pallas_call(body, out_shape=outs, in_specs=[vmem] * len(arrays) + [rem...  6.92 us

profile of v6, /device:TPU:1, one launch (start us, length us, event | category | flops | bytes accessed | tf_op | source)
XLA Modules:
  0.0 143.4 jit_solution(450225905343130181)
XLA Ops:
  0.6 0.0 copy-start.8
  0.6 0.0 copy-start.9
  0.7 0.0 copy-start.4
  0.7 1.8 %shard_map.131 = bf16[16,40,128]{2,1,0:T(8,128)(2,1)} custom-call(bf16[16,16]{1,0:T(8,128)(2,1)} %query.1, bf16[16,4096]{1,0:T(8,128)(2,1)} %out_proj.1), custom_call_target="tpu_custom_call" | custom-call | tf_op jit(solution)/shard_map/pallas_call | solution.py:301
  2.4 0.0 copy-start.3
  2.4 28.1 %all_to_all.40.arrived.dealt = bf16[16,40,128]{2,1,0:T(8,128)(2,1)S(1)} all-to-all(bf16[16,40,128]{2,1,0:T(8,128)(2,1)} %shard_map.131), channel_id=1, replica_groups=mesh['x'=4,'z'=16,'c'=2,'y'=4] {'z'}, dimensions={0} | all-to-all | bytes 327680 | tf_op jit(solution)/shard_map/all_to_all | solution.py:312
  30.6 0.0 copy-done.8
  30.6 0.0 copy-done.9
  30.6 0.2 shard_map.132
  30.8 20.1 %all_to_all.41.gathered = bf16[32,32,128]{2,1,0:T(8,128)(2,1)S(1)} all-to-all(bf16[32,32,128]{2,1,0:T(8,128)(2,1)S(1)} %get-tuple-element.10), channel_id=1, replica_groups=mesh['x'=4,'z'=16,'c'=2,'y'=4] {'x','c','y'}, dimensions={0} | all-to-all | bytes 524288 | tf_op jit(solution)/shard_map/all_to_all | solution.py:312
  50.8 0.0 copy-done.4
  50.8 0.0 copy-done.3
  50.8 0.0 copy-start.2
  50.8 0.8 shard_map.133
  51.7 0.0 copy-start.1
  51.7 13.5 %all_to_all.42.arrived = bf16[32,40,128]{2,1,0:T(8,128)(2,1)S(1)} all-to-all(bf16[32,40,128]{2,1,0:T(8,128)(2,1)S(1)} %shard_map.133), channel_id=1, replica_groups=mesh['x'=4,'z'=16,'c'=2,'y'=4] {'x','c','y'}, dimensions={0} | all-to-all | bytes 655360 | tf_op jit(solution)/shard_map/all_to_all | solution.py:312
  65.2 0.0 copy-start
  65.2 0.3 shard_map.134
  65.5 16.0 %all_to_all.43.arrived = bf16[16,40,128]{2,1,0:T(8,128)(2,1)S(1)} all-to-all(bf16[16,40,128]{2,1,0:T(8,128)(2,1)S(1)} %get-tuple-element.12), channel_id=1, replica_groups=mesh['x'=4,'z'=16,'c'=2,'y'=4] {'z'}, dimensions={0} | all-to-all | bytes 327680 | tf_op jit(solution)/shard_map/all_to_all | solution.py:312
  81.6 0.8 shard_map.135
  82.4 0.0 copy-start.5
  82.4 16.3 %all_to_all.44.arrived = bf16[32,16,256]{2,1,0:T(8,128)(2,1)S(1)} all-to-all(bf16[32,16,256]{2,1,0:T(8,128)(2,1)S(1)} %get-tuple-element.14), channel_id=1, replica_groups=mesh['x'=4,'z'=16,'c'=2,'y'=4] {'x','c','y'}, dimensions={0} | all-to-all | bytes 524288 | tf_op jit(solution)/shard_map/all_to_all | solution.py:312
  98.6 0.0 copy-done.5
  98.6 0.3 shard_map.136
  99.0 0.0 copy-start.6
  99.0 0.0 copy-start.7
  99.0 15.3 %all_to_all.45.arrived = bf16[16,8,128]{2,1,0:T(8,128)(2,1)S(1)} all-to-all(bf16[16,8,128]{2,1,0:T(8,128)(2,1)S(1)} %get-tuple-element.16), channel_id=1, replica_groups=mesh['x'=4,'z'=16,'c'=2,'y'=4] {'z'}, dimensions={0} | all-to-all | bytes 65536 | tf_op jit(solution)/shard_map/all_to_all | solution.py:312
  114.3 0.0 copy-done.2
  114.3 0.0 copy-done.1
  114.3 0.0 copy-done
  114.3 0.0 copy-done.6
  114.3 0.0 copy-done.7
  114.3 1.5 %shard_map.137 = bf16[32,4,128]{2,1,0:T(4,128)(2,1)S(1)} custom-call(bf16[16,8,128]{2,1,0:T(8,128)(2,1)S(1)} %all_to_all.45.arrived, bf16[32,128]{1,0:T(8,128)(2,1)S(1)} %bitcast.9, s32[8,16]{1,0:T(8,128)S(1)} %bitcast.7, f32[8,16]{1,0:T(8,128)S(1)} %bitcast.10, bf16[128,4096]{1,0:T(8,128)(2,1)S(1)} %copy-done, bf16[128,4096]{1,0:T(8,128)(2,1)S(1)} %copy-done.1, ...), custom_call_target="tpu_custom_call" | custom-call | tf_op jit(solution)/shard_map/pallas_call | solution.py:301
  115.8 12.6 %all_to_all.46.arrived = bf16[32,4,128]{2,1,0:T(4,128)(2,1)S(1)} all-to-all(bf16[32,4,128]{2,1,0:T(4,128)(2,1)S(1)} %shard_map.137), channel_id=1, replica_groups=mesh['x'=4,'z'=16,'c'=2,'y'=4] {'x','c','y'}, dimensions={0} | all-to-all | bytes 65536 | tf_op jit(solution)/shard_map/all_to_all | solution.py:312
  128.3 0.5 shard_map.138
  128.8 13.8 %all_to_all.47.arrived = bf16[16,1,128]{2,1,0:T(2,128)(2,1)S(1)} all-to-all(bf16[16,1,128]{2,1,0:T(2,128)(2,1)S(1)} %shard_map.138), channel_id=1, replica_groups=mesh['x'=4,'z'=16,'c'=2,'y'=4] {'z'}, dimensions={0} | all-to-all | bytes 8192 | tf_op jit(solution)/shard_map/all_to_all | solution.py:312
  142.6 0.8 shard_map.139
Async XLA Ops:
  0.6 29.9 %copy-start.8 = (bf16[16,8]{0,1:T(8,128)(2,1)S(1)}, bf16[16,8]{0,1:T(8,128)(2,1)}, u32[]{:S(2)}) copy-start(bf16[16,8]{0,1:T(8,128)(2,1)} %param.16) | copy-start | bytes 772
  0.6 29.9 %copy-start.9 = (s32[16]{0:T(128)S(1)}, s32[16]{0:T(128)}, u32[]{:S(2)}) copy-start(s32[16]{0:T(128)} %param.15) | copy-start | bytes 196
  0.7 50.2 %copy-start.4 = (bf16[16,32,512]{2,1,0:T(8,128)(2,1)S(1)}, bf16[16,32,512]{2,1,0:T(8,128)(2,1)}, u32[]{:S(2)}) copy-start(bf16[16,32,512]{2,1,0:T(8,128)(2,1)} %values.1) | copy-start | bytes 1572868
  2.4 48.4 %copy-start.3 = (bf16[16,32,512]{2,1,0:T(8,128)(2,1)S(1)}, bf16[16,32,512]{2,1,0:T(8,128)(2,1)}, u32[]{:S(2)}) copy-start(bf16[16,32,512]{2,1,0:T(8,128)(2,1)} %keys.1) | copy-start | bytes 1572868
  50.8 63.5 %copy-start.2 = (bf16[128,4096]{1,0:T(8,128)(2,1)S(1)}, bf16[128,4096]{1,0:T(8,128)(2,1)}, u32[]{:S(2)}) copy-start(bf16[128,4096]{1,0:T(8,128)(2,1)} %w_down.1) | copy-start | bytes 3145732
  51.7 62.6 %copy-start.1 = (bf16[128,4096]{1,0:T(8,128)(2,1)S(1)}, bf16[128,4096]{1,0:T(8,128)(2,1)}, u32[]{:S(2)}) copy-start(bf16[128,4096]{1,0:T(8,128)(2,1)} %w_up.1) | copy-start | bytes 3145732
  65.2 49.1 %copy-start = (bf16[128,4096]{1,0:T(8,128)(2,1)S(1)}, bf16[128,4096]{1,0:T(8,128)(2,1)}, u32[]{:S(2)}) copy-start(bf16[128,4096]{1,0:T(8,128)(2,1)} %w_gate.1) | copy-start | bytes 3145732
  82.4 16.3 %copy-start.5 = (s32[16,8]{0,1:T(8,128)S(1)}, s32[16,8]{0,1:T(8,128)}, u32[]{:S(2)}) copy-start(s32[16,8]{0,1:T(8,128)} %param.19) | copy-start | bytes 1540
  99.0 15.3 %copy-start.6 = (bf16[4096]{0:T(1024)(128)(2,1)S(1)}, bf16[4096]{0:T(1024)(128)(2,1)}, u32[]{:S(2)}) copy-start(bf16[4096]{0:T(1024)(128)(2,1)} %param.18) | copy-start | bytes 24580
  99.0 15.3 %copy-start.7 = (f32[16,8]{0,1:T(8,128)S(1)}, f32[16,8]{0,1:T(8,128)}, u32[]{:S(2)}) copy-start(f32[16,8]{0,1:T(8,128)} %param.20) | copy-start | bytes 1540

commit v7 on v5

--- a/solution.py
+++ b/solution.py
@@ -268,7 +268,7 @@
         start = group * 1024
         tiles = [weighted[:, start + v * 128 : start + (v + 1) * 128] for v in range(8)]
         for c, tile in enumerate(sort_columns(tiles)):
-            out[group * CY + c] = tile.astype(BF)
+            out[group * CY + c] = tile[:4].astype(BF)
 
 
 def sum_experts(arrived, expert_ids, out):
@@ -276,14 +276,15 @@
     parts = [
         jnp.sum(arrived[x * CY : (x + 1) * CY].astype(F32), axis=0) for x in range(X)
     ]
-    row = iota((8 * X, B), 0)
-    table = slots(expert_ids[...], row // 8 * Z + z, row % 8).astype(F32)
+    row = iota((4 * X, B), 0)
+    table = slots(expert_ids[...], row // 4 * Z + z, row % 4).astype(F32)
     turned = dot(jnp.concatenate(parts, axis=0), table, ((0,), (0,)), EXACT)
     out[...] = turned.reshape(Z, 8, B).astype(BF)
 
 
-def finish_layer(arrived, mid_part, out):
+def finish_layer(arrived, mid_part, context, out, context_out):
     out[...] = (mid_part[...] + jnp.sum(arrived[...].astype(F32), axis=0)).astype(BF)
+    context_out[...] = context[...]
 
 
 def call(body, outs, arrays, far=(), scratch=(), limit=16):
@@ -362,11 +363,13 @@
     )
     mixture = call(
         experts,
-        shape(PLANE, 8, 128),
+        shape(PLANE, 4, 128),
         (swap(picked, "z"), norm_gain.reshape(PLANE, 128), ids, routes, w_gate, w_up, w_down),
     )
     summed = call(sum_experts, shape(Z, 8, B), (swap(mixture, PLANE_AXES), ids))
-    layer_out = call(finish_layer, shape(8, B), (swap(summed, "z"), mid_part))
+    layer_out, context = call(
+        finish_layer, [shape(8, B), shape(B, 16)], (swap(summed, "z"), mid_part, context)
+    )
     return context, layer_out.T
 
 

time: 144 us -> 143 us (level)
  no operation moved by 1% of the time
where the time goes in v7:
time: 143 us
  blocking collectives  136 us (95%)
  Pallas kernels  6.24 us (4%)
    all_to_all x8, blocking collectives, swap(): return lax.all_to_all(blocks, axes, 0, 0, tiled=True)  136 us
    pallas_call x9, Pallas kernels, call(): pl.pallas_call(body, out_shape=outs, in_specs=[vmem] * len(arrays) + [rem...  6.24 us

profile of v7, /device:TPU:1, one launch (start us, length us, event | category | flops | bytes accessed | tf_op | source)
XLA Modules:
  0.0 142.9 jit_solution(6449415111364331212)
XLA Ops:
  0.6 0.0 copy-start.8
  0.6 0.0 copy-start.9
  0.7 0.0 copy-start.4
  0.7 1.8 %shard_map.131 = bf16[16,40,128]{2,1,0:T(8,128)(2,1)} custom-call(bf16[16,16]{1,0:T(8,128)(2,1)} %query.1, bf16[16,4096]{1,0:T(8,128)(2,1)} %out_proj.1), custom_call_target="tpu_custom_call" | custom-call | tf_op jit(solution)/shard_map/pallas_call | solution.py:294
  2.4 0.0 copy-start.3
  2.4 28.1 %all_to_all.40.arrived.dealt = bf16[16,40,128]{2,1,0:T(8,128)(2,1)S(1)} all-to-all(bf16[16,40,128]{2,1,0:T(8,128)(2,1)} %shard_map.131), channel_id=1, replica_groups=mesh['x'=4,'z'=16,'c'=2,'y'=4] {'z'}, dimensions={0} | all-to-all | bytes 327680 | tf_op jit(solution)/shard_map/all_to_all | solution.py:305
  30.6 0.0 copy-done.8
  30.6 0.0 copy-done.9
  30.6 0.2 shard_map.132
  30.8 20.1 %all_to_all.41.gathered = bf16[32,32,128]{2,1,0:T(8,128)(2,1)S(1)} all-to-all(bf16[32,32,128]{2,1,0:T(8,128)(2,1)S(1)} %get-tuple-element.12), channel_id=1, replica_groups=mesh['x'=4,'z'=16,'c'=2,'y'=4] {'x','c','y'}, dimensions={0} | all-to-all | bytes 524288 | tf_op jit(solution)/shard_map/all_to_all | solution.py:305
  50.8 0.0 copy-done.4
  50.8 0.0 copy-done.3
  50.8 0.0 copy-start.2
  50.8 0.8 shard_map.133
  51.7 0.0 copy-start.1
  51.7 13.5 %all_to_all.42.arrived = bf16[32,40,128]{2,1,0:T(8,128)(2,1)S(1)} all-to-all(bf16[32,40,128]{2,1,0:T(8,128)(2,1)S(1)} %shard_map.133), channel_id=1, replica_groups=mesh['x'=4,'z'=16,'c'=2,'y'=4] {'x','c','y'}, dimensions={0} | all-to-all | bytes 655360 | tf_op jit(solution)/shard_map/all_to_all | solution.py:305
  65.2 0.0 copy-start
  65.2 0.3 shard_map.134
  65.5 16.0 %all_to_all.43.arrived = bf16[16,40,128]{2,1,0:T(8,128)(2,1)S(1)} all-to-all(bf16[16,40,128]{2,1,0:T(8,128)(2,1)S(1)} %get-tuple-element.14), channel_id=1, replica_groups=mesh['x'=4,'z'=16,'c'=2,'y'=4] {'z'}, dimensions={0} | all-to-all | bytes 327680 | tf_op jit(solution)/shard_map/all_to_all | solution.py:305
  81.6 0.4 shard_map.135
  82.0 0.0 copy-start.5
  82.0 16.1 %all_to_all.44.arrived = bf16[32,16,256]{2,1,0:T(8,128)(2,1)S(1)} all-to-all(bf16[32,16,256]{2,1,0:T(8,128)(2,1)S(1)} %get-tuple-element.15), channel_id=1, replica_groups=mesh['x'=4,'z'=16,'c'=2,'y'=4] {'x','c','y'}, dimensions={0} | all-to-all | bytes 524288 | tf_op jit(solution)/shard_map/all_to_all | solution.py:305
  98.1 0.0 copy-done.5
  98.1 0.3 shard_map.136
  98.5 0.0 copy-start.6
  98.5 0.0 copy-start.7
  98.5 15.3 %all_to_all.45.arrived = bf16[16,8,128]{2,1,0:T(8,128)(2,1)S(1)} all-to-all(bf16[16,8,128]{2,1,0:T(8,128)(2,1)S(1)} %get-tuple-element.17), channel_id=1, replica_groups=mesh['x'=4,'z'=16,'c'=2,'y'=4] {'z'}, dimensions={0} | all-to-all | bytes 65536 | tf_op jit(solution)/shard_map/all_to_all | solution.py:305
  113.8 0.0 copy-done.2
  113.8 0.0 copy-done.1
  113.8 0.0 copy-done
  113.8 0.0 copy-done.6
  113.8 0.0 copy-done.7
  113.8 1.5 %shard_map.137 = bf16[32,4,128]{2,1,0:T(4,128)(2,1)S(1)} custom-call(bf16[16,8,128]{2,1,0:T(8,128)(2,1)S(1)} %all_to_all.45.arrived, bf16[32,128]{1,0:T(8,128)(2,1)S(1)} %bitcast.9, s32[8,16]{1,0:T(8,128)S(1)} %bitcast.7, f32[8,16]{1,0:T(8,128)S(1)} %bitcast.10, bf16[128,4096]{1,0:T(8,128)(2,1)S(1)} %copy-done, bf16[128,4096]{1,0:T(8,128)(2,1)S(1)} %copy-done.1, ...), custom_call_target="tpu_custom_call" | custom-call | tf_op jit(solution)/shard_map/pallas_call | solution.py:294
  115.3 12.6 %all_to_all.46.arrived = bf16[32,4,128]{2,1,0:T(4,128)(2,1)S(1)} all-to-all(bf16[32,4,128]{2,1,0:T(4,128)(2,1)S(1)} %shard_map.137), channel_id=1, replica_groups=mesh['x'=4,'z'=16,'c'=2,'y'=4] {'x','c','y'}, dimensions={0} | all-to-all | bytes 65536 | tf_op jit(solution)/shard_map/all_to_all | solution.py:305
  127.9 0.3 shard_map.138
  128.2 14.1 %all_to_all.47.arrived = bf16[16,8,16]{2,1,0:T(8,128)(2,1)S(1)} all-to-all(bf16[16,8,16]{2,1,0:T(8,128)(2,1)S(1)} %shard_map.138), channel_id=1, replica_groups=mesh['x'=4,'z'=16,'c'=2,'y'=4] {'z'}, dimensions={0} | all-to-all | bytes 8192 | tf_op jit(solution)/shard_map/all_to_all | solution.py:305
  142.3 0.6 shard_map.139
Async XLA Ops:
  0.6 29.9 %copy-start.8 = (bf16[16,8]{0,1:T(8,128)(2,1)S(1)}, bf16[16,8]{0,1:T(8,128)(2,1)}, u32[]{:S(2)}) copy-start(bf16[16,8]{0,1:T(8,128)(2,1)} %param.16) | copy-start | bytes 772
  0.6 29.9 %copy-start.9 = (s32[16]{0:T(128)S(1)}, s32[16]{0:T(128)}, u32[]{:S(2)}) copy-start(s32[16]{0:T(128)} %param.15) | copy-start | bytes 196
  0.7 50.2 %copy-start.4 = (bf16[16,32,512]{2,1,0:T(8,128)(2,1)S(1)}, bf16[16,32,512]{2,1,0:T(8,128)(2,1)}, u32[]{:S(2)}) copy-start(bf16[16,32,512]{2,1,0:T(8,128)(2,1)} %values.1) | copy-start | bytes 1572868
  2.4 48.4 %copy-start.3 = (bf16[16,32,512]{2,1,0:T(8,128)(2,1)S(1)}, bf16[16,32,512]{2,1,0:T(8,128)(2,1)}, u32[]{:S(2)}) copy-start(bf16[16,32,512]{2,1,0:T(8,128)(2,1)} %keys.1) | copy-start | bytes 1572868
  50.8 63.0 %copy-start.2 = (bf16[128,4096]{1,0:T(8,128)(2,1)S(1)}, bf16[128,4096]{1,0:T(8,128)(2,1)}, u32[]{:S(2)}) copy-start(bf16[128,4096]{1,0:T(8,128)(2,1)} %w_down.1) | copy-start | bytes 3145732
  51.7 62.2 %copy-start.1 = (bf16[128,4096]{1,0:T(8,128)(2,1)S(1)}, bf16[128,4096]{1,0:T(8,128)(2,1)}, u32[]{:S(2)}) copy-start(bf16[128,4096]{1,0:T(8,128)(2,1)} %w_up.1) | copy-start | bytes 3145732
  65.2 48.6 %copy-start = (bf16[128,4096]{1,0:T(8,128)(2,1)S(1)}, bf16[128,4096]{1,0:T(8,128)(2,1)}, u32[]{:S(2)}) copy-start(bf16[128,4096]{1,0:T(8,128)(2,1)} %w_gate.1) | copy-start | bytes 3145732
  82.0 16.1 %copy-start.5 = (s32[16,8]{0,1:T(8,128)S(1)}, s32[16,8]{0,1:T(8,128)}, u32[]{:S(2)}) copy-start(s32[16,8]{0,1:T(8,128)} %param.19) | copy-start | bytes 1540
  98.5 15.3 %copy-start.6 = (bf16[4096]{0:T(1024)(128)(2,1)S(1)}, bf16[4096]{0:T(1024)(128)(2,1)}, u32[]{:S(2)}) copy-start(bf16[4096]{0:T(1024)(128)(2,1)} %param.18) | copy-start | bytes 24580
  98.5 15.3 %copy-start.7 = (f32[16,8]{0,1:T(8,128)S(1)}, f32[16,8]{0,1:T(8,128)}, u32[]{:S(2)}) copy-start(f32[16,8]{0,1:T(8,128)} %param.20) | copy-start | bytes 1540

commit v8 on v7

--- a/solution.py
+++ b/solution.py
@@ -328,7 +328,7 @@
     dealt = swap(
         call(
             deal_out,
-            shape(Z, 40, 128),
+            vmem((Z, 40, 128), BF),
             (),
             (query, out_proj),
             (vmem((B, 16), BF), vmem((16, D), BF), dma((2,))),

time: 143 us -> 142 us (level)
  no operation moved by 1% of the time
where the time goes in v8:
time: 142 us
  blocking collectives  136 us (96%)
  Pallas kernels  5.58 us (4%)
    all_to_all x8, blocking collectives, swap(): return lax.all_to_all(blocks, axes, 0, 0, tiled=True)  136 us
    pallas_call x9, Pallas kernels, call(): pl.pallas_call(body, out_shape=outs, in_specs=[vmem] * len(arrays) + [rem...  5.58 us

profile of v8, /device:TPU:1, one launch (start us, length us, event | category | flops | bytes accessed | tf_op | source)
XLA Modules:
  0.0 142.0 jit_solution(12992847083281747482)
XLA Ops:
  0.6 0.0 copy-start.8
  0.6 0.0 copy-start.9
  0.7 0.0 copy-start.4
  0.7 1.1 shard_map.131
  1.8 0.0 copy-start.3
  1.8 27.9 %all_to_all.40.arrived.dealt = bf16[16,40,128]{2,1,0:T(8,128)(2,1)S(1)} all-to-all(bf16[16,40,128]{2,1,0:T(8,128)(2,1)S(1)} %shard_map.131), channel_id=1, replica_groups=mesh['x'=4,'z'=16,'c'=2,'y'=4] {'z'}, dimensions={0} | all-to-all | bytes 327680 | tf_op jit(solution)/shard_map/all_to_all | solution.py:305
  29.7 0.0 copy-done.8
  29.7 0.0 copy-done.9
  29.7 0.2 shard_map.132
  29.9 20.1 %all_to_all.41.gathered = bf16[32,32,128]{2,1,0:T(8,128)(2,1)S(1)} all-to-all(bf16[32,32,128]{2,1,0:T(8,128)(2,1)S(1)} %get-tuple-element.12), channel_id=1, replica_groups=mesh['x'=4,'z'=16,'c'=2,'y'=4] {'x','c','y'}, dimensions={0} | all-to-all | bytes 524288 | tf_op jit(solution)/shard_map/all_to_all | solution.py:305
  49.9 0.0 copy-done.4
  49.9 0.0 copy-done.3
  49.9 0.0 copy-start.2
  50.0 0.8 shard_map.133
  50.8 0.0 copy-start.1
  50.8 13.5 %all_to_all.42.arrived = bf16[32,40,128]{2,1,0:T(8,128)(2,1)S(1)} all-to-all(bf16[32,40,128]{2,1,0:T(8,128)(2,1)S(1)} %shard_map.133), channel_id=1, replica_groups=mesh['x'=4,'z'=16,'c'=2,'y'=4] {'x','c','y'}, dimensions={0} | all-to-all | bytes 655360 | tf_op jit(solution)/shard_map/all_to_all | solution.py:305
  64.3 0.0 copy-start
  64.3 0.3 shard_map.134
  64.6 16.0 %all_to_all.43.arrived = bf16[16,40,128]{2,1,0:T(8,128)(2,1)S(1)} all-to-all(bf16[16,40,128]{2,1,0:T(8,128)(2,1)S(1)} %get-tuple-element.14), channel_id=1, replica_groups=mesh['x'=4,'z'=16,'c'=2,'y'=4] {'z'}, dimensions={0} | all-to-all | bytes 327680 | tf_op jit(solution)/shard_map/all_to_all | solution.py:305
  80.7 0.4 shard_map.135
  81.1 0.0 copy-start.5
  81.1 16.1 %all_to_all.44.arrived = bf16[32,16,256]{2,1,0:T(8,128)(2,1)S(1)} all-to-all(bf16[32,16,256]{2,1,0:T(8,128)(2,1)S(1)} %get-tuple-element.15), channel_id=1, replica_groups=mesh['x'=4,'z'=16,'c'=2,'y'=4] {'x','c','y'}, dimensions={0} | all-to-all | bytes 524288 | tf_op jit(solution)/shard_map/all_to_all | solution.py:305
  97.3 0.0 copy-done.5
  97.3 0.3 shard_map.136
  97.6 0.0 copy-start.6
  97.6 0.0 copy-start.7
  97.6 15.3 %all_to_all.45.arrived = bf16[16,8,128]{2,1,0:T(8,128)(2,1)S(1)} all-to-all(bf16[16,8,128]{2,1,0:T(8,128)(2,1)S(1)} %get-tuple-element.17), channel_id=1, replica_groups=mesh['x'=4,'z'=16,'c'=2,'y'=4] {'z'}, dimensions={0} | all-to-all | bytes 65536 | tf_op jit(solution)/shard_map/all_to_all | solution.py:305
  112.9 0.0 copy-done.2
  112.9 0.0 copy-done.1
  112.9 0.0 copy-done
  112.9 0.0 copy-done.6
  113.0 0.0 copy-done.7
  113.0 1.5 %shard_map.137 = bf16[32,4,128]{2,1,0:T(4,128)(2,1)S(1)} custom-call(bf16[16,8,128]{2,1,0:T(8,128)(2,1)S(1)} %all_to_all.45.arrived, bf16[32,128]{1,0:T(8,128)(2,1)S(1)} %bitcast.9, s32[8,16]{1,0:T(8,128)S(1)} %bitcast.7, f32[8,16]{1,0:T(8,128)S(1)} %bitcast.10, bf16[128,4096]{1,0:T(8,128)(2,1)S(1)} %copy-done, bf16[128,4096]{1,0:T(8,128)(2,1)S(1)} %copy-done.1, ...), custom_call_target="tpu_custom_call" | custom-call | tf_op jit(solution)/shard_map/pallas_call | solution.py:294
  114.4 12.6 %all_to_all.46.arrived = bf16[32,4,128]{2,1,0:T(4,128)(2,1)S(1)} all-to-all(bf16[32,4,128]{2,1,0:T(4,128)(2,1)S(1)} %shard_map.137), channel_id=1, replica_groups=mesh['x'=4,'z'=16,'c'=2,'y'=4] {'x','c','y'}, dimensions={0} | all-to-all | bytes 65536 | tf_op jit(solution)/shard_map/all_to_all | solution.py:305
  127.0 0.3 shard_map.138
  127.3 14.1 %all_to_all.47.arrived = bf16[16,8,16]{2,1,0:T(8,128)(2,1)S(1)} all-to-all(bf16[16,8,16]{2,1,0:T(8,128)(2,1)S(1)} %shard_map.138), channel_id=1, replica_groups=mesh['x'=4,'z'=16,'c'=2,'y'=4] {'z'}, dimensions={0} | all-to-all | bytes 8192 | tf_op jit(solution)/shard_map/all_to_all | solution.py:305
  141.4 0.6 shard_map.139
Async XLA Ops:
  0.6 29.0 %copy-start.8 = (bf16[16,8]{0,1:T(8,128)(2,1)S(1)}, bf16[16,8]{0,1:T(8,128)(2,1)}, u32[]{:S(2)}) copy-start(bf16[16,8]{0,1:T(8,128)(2,1)} %param.16) | copy-start | bytes 772
  0.6 29.0 %copy-start.9 = (s32[16]{0:T(128)S(1)}, s32[16]{0:T(128)}, u32[]{:S(2)}) copy-start(s32[16]{0:T(128)} %param.15) | copy-start | bytes 196
  0.7 49.3 %copy-start.4 = (bf16[16,32,512]{2,1,0:T(8,128)(2,1)S(1)}, bf16[16,32,512]{2,1,0:T(8,128)(2,1)}, u32[]{:S(2)}) copy-start(bf16[16,32,512]{2,1,0:T(8,128)(2,1)} %values.1) | copy-start | bytes 1572868
  1.8 48.2 %copy-start.3 = (bf16[16,32,512]{2,1,0:T(8,128)(2,1)S(1)}, bf16[16,32,512]{2,1,0:T(8,128)(2,1)}, u32[]{:S(2)}) copy-start(bf16[16,32,512]{2,1,0:T(8,128)(2,1)} %keys.1) | copy-start | bytes 1572868
  49.9 63.0 %copy-start.2 = (bf16[128,4096]{1,0:T(8,128)(2,1)S(1)}, bf16[128,4096]{1,0:T(8,128)(2,1)}, u32[]{:S(2)}) copy-start(bf16[128,4096]{1,0:T(8,128)(2,1)} %w_down.1) | copy-start | bytes 3145732
  50.8 62.2 %copy-start.1 = (bf16[128,4096]{1,0:T(8,128)(2,1)S(1)}, bf16[128,4096]{1,0:T(8,128)(2,1)}, u32[]{:S(2)}) copy-start(bf16[128,4096]{1,0:T(8,128)(2,1)} %w_up.1) | copy-start | bytes 3145732
  64.3 48.6 %copy-start = (bf16[128,4096]{1,0:T(8,128)(2,1)S(1)}, bf16[128,4096]{1,0:T(8,128)(2,1)}, u32[]{:S(2)}) copy-start(bf16[128,4096]{1,0:T(8,128)(2,1)} %w_gate.1) | copy-start | bytes 3145732
  81.1 16.1 %copy-start.5 = (s32[16,8]{0,1:T(8,128)S(1)}, s32[16,8]{0,1:T(8,128)}, u32[]{:S(2)}) copy-start(s32[16,8]{0,1:T(8,128)} %param.19) | copy-start | bytes 1540
  97.6 15.3 %copy-start.6 = (bf16[4096]{0:T(1024)(128)(2,1)S(1)}, bf16[4096]{0:T(1024)(128)(2,1)}, u32[]{:S(2)}) copy-start(bf16[4096]{0:T(1024)(128)(2,1)} %param.18) | copy-start | bytes 24580
  97.6 15.3 %copy-start.7 = (f32[16,8]{0,1:T(8,128)S(1)}, f32[16,8]{0,1:T(8,128)}, u32[]{:S(2)}) copy-start(f32[16,8]{0,1:T(8,128)} %param.20) | copy-start | bytes 1540

commit v9 on v8

--- a/solution.py
+++ b/solution.py
@@ -51,10 +51,12 @@
 
 
 def deal_out(query, out_proj, out, held_query, held, sems):
-    copies = [
-        pltpu.make_async_copy(query, held_query, sems.at[0]),
-        pltpu.make_async_copy(out_proj, held, sems.at[1]),
-    ]
+    copies = [pltpu.make_async_copy(query, held_query, sems.at[0])]
+    for x in range(X):
+        part = pl.ds(x * 1024, 1024)
+        copies.append(
+            pltpu.make_async_copy(out_proj.at[:, part], held.at[:, part], sems.at[1 + x])
+        )
     for copy in copies:
         copy.start()
     copies[0].wait()
@@ -64,7 +66,8 @@
         put = (iota((16, 128), 0) + i * 16 == iota((16, 128), 1)).astype(BF)
         parts.append(dot(own, put, ((1,), (0,)))[i * 8 : (i + 1) * 8])
     wide = (parts[0] + parts[1]).astype(BF)
-    copies[1].wait()
+    for copy in copies[1:]:
+        copy.wait()
     for v in range(Z // 2):
         tiles = [
             held[:, x * 1024 + v * 128 : x * 1024 + (v + 1) * 128] for x in range(X)
@@ -331,7 +334,7 @@
             vmem((Z, 40, 128), BF),
             (),
             (query, out_proj),
-            (vmem((B, 16), BF), vmem((16, D), BF), dma((2,))),
+            (vmem((B, 16), BF), vmem((16, D), BF), dma((1 + X,))),
             62,
         ),
         "z",

time: 142 us -> 142 us (level)
  no operation moved by 1% of the time
where the time goes in v9:
time: 142 us
  blocking collectives  136 us (96%)
  Pallas kernels  5.5 us (4%)
    all_to_all x8, blocking collectives, swap(): return lax.all_to_all(blocks, axes, 0, 0, tiled=True)  136 us
    pallas_call x9, Pallas kernels, call(): pl.pallas_call(body, out_shape=outs, in_specs=[vmem] * len(arrays) + [rem...  5.5 us

profile of v9, /device:TPU:1, one launch (start us, length us, event | category | flops | bytes accessed | tf_op | source)
XLA Modules:
  0.0 141.9 jit_solution(13391601429362560173)
XLA Ops:
  0.6 0.0 copy-start.8
  0.6 0.0 copy-start.9
  0.7 0.0 copy-start.4
  0.7 1.0 shard_map.131
  1.7 0.0 copy-start.3
  1.7 27.9 %all_to_all.40.arrived.dealt = bf16[16,40,128]{2,1,0:T(8,128)(2,1)S(1)} all-to-all(bf16[16,40,128]{2,1,0:T(8,128)(2,1)S(1)} %shard_map.131), channel_id=1, replica_groups=mesh['x'=4,'z'=16,'c'=2,'y'=4] {'z'}, dimensions={0} | all-to-all | bytes 327680 | tf_op jit(solution)/shard_map/all_to_all | solution.py:308
  29.6 0.0 copy-done.8
  29.6 0.0 copy-done.9
  29.6 0.2 shard_map.132
  29.8 20.1 %all_to_all.41.gathered = bf16[32,32,128]{2,1,0:T(8,128)(2,1)S(1)} all-to-all(bf16[32,32,128]{2,1,0:T(8,128)(2,1)S(1)} %get-tuple-element.12), channel_id=1, replica_groups=mesh['x'=4,'z'=16,'c'=2,'y'=4] {'x','c','y'}, dimensions={0} | all-to-all | bytes 524288 | tf_op jit(solution)/shard_map/all_to_all | solution.py:308
  49.9 0.0 copy-done.4
  49.9 0.0 copy-done.3
  49.9 0.0 copy-start.2
  49.9 0.8 shard_map.133
  50.7 0.0 copy-start.1
  50.7 13.5 %all_to_all.42.arrived = bf16[32,40,128]{2,1,0:T(8,128)(2,1)S(1)} all-to-all(bf16[32,40,128]{2,1,0:T(8,128)(2,1)S(1)} %shard_map.133), channel_id=1, replica_groups=mesh['x'=4,'z'=16,'c'=2,'y'=4] {'x','c','y'}, dimensions={0} | all-to-all | bytes 655360 | tf_op jit(solution)/shard_map/all_to_all | solution.py:308
  64.2 0.0 copy-start
  64.2 0.3 shard_map.134
  64.6 16.0 %all_to_all.43.arrived = bf16[16,40,128]{2,1,0:T(8,128)(2,1)S(1)} all-to-all(bf16[16,40,128]{2,1,0:T(8,128)(2,1)S(1)} %get-tuple-element.14), channel_id=1, replica_groups=mesh['x'=4,'z'=16,'c'=2,'y'=4] {'z'}, dimensions={0} | all-to-all | bytes 327680 | tf_op jit(solution)/shard_map/all_to_all | solution.py:308
  80.6 0.4 shard_map.135
  81.1 0.0 copy-start.5
  81.1 16.1 %all_to_all.44.arrived = bf16[32,16,256]{2,1,0:T(8,128)(2,1)S(1)} all-to-all(bf16[32,16,256]{2,1,0:T(8,128)(2,1)S(1)} %get-tuple-element.15), channel_id=1, replica_groups=mesh['x'=4,'z'=16,'c'=2,'y'=4] {'x','c','y'}, dimensions={0} | all-to-all | bytes 524288 | tf_op jit(solution)/shard_map/all_to_all | solution.py:308
  97.2 0.0 copy-done.5
  97.2 0.3 shard_map.136
  97.5 0.0 copy-start.6
  97.5 0.0 copy-start.7
  97.5 15.3 %all_to_all.45.arrived = bf16[16,8,128]{2,1,0:T(8,128)(2,1)S(1)} all-to-all(bf16[16,8,128]{2,1,0:T(8,128)(2,1)S(1)} %get-tuple-element.17), channel_id=1, replica_groups=mesh['x'=4,'z'=16,'c'=2,'y'=4] {'z'}, dimensions={0} | all-to-all | bytes 65536 | tf_op jit(solution)/shard_map/all_to_all | solution.py:308
  112.9 0.0 copy-done.2
  112.9 0.0 copy-done.1
  112.9 0.0 copy-done
  112.9 0.0 copy-done.6
  112.9 0.0 copy-done.7
  112.9 1.5 %shard_map.137 = bf16[32,4,128]{2,1,0:T(4,128)(2,1)S(1)} custom-call(bf16[16,8,128]{2,1,0:T(8,128)(2,1)S(1)} %all_to_all.45.arrived, bf16[32,128]{1,0:T(8,128)(2,1)S(1)} %bitcast.9, s32[8,16]{1,0:T(8,128)S(1)} %bitcast.7, f32[8,16]{1,0:T(8,128)S(1)} %bitcast.10, bf16[128,4096]{1,0:T(8,128)(2,1)S(1)} %copy-done, bf16[128,4096]{1,0:T(8,128)(2,1)S(1)} %copy-done.1, ...), custom_call_target="tpu_custom_call" | custom-call | tf_op jit(solution)/shard_map/pallas_call | solution.py:297
  114.4 12.6 %all_to_all.46.arrived = bf16[32,4,128]{2,1,0:T(4,128)(2,1)S(1)} all-to-all(bf16[32,4,128]{2,1,0:T(4,128)(2,1)S(1)} %shard_map.137), channel_id=1, replica_groups=mesh['x'=4,'z'=16,'c'=2,'y'=4] {'x','c','y'}, dimensions={0} | all-to-all | bytes 65536 | tf_op jit(solution)/shard_map/all_to_all | solution.py:308
  126.9 0.3 shard_map.138
  127.2 14.1 %all_to_all.47.arrived = bf16[16,8,16]{2,1,0:T(8,128)(2,1)S(1)} all-to-all(bf16[16,8,16]{2,1,0:T(8,128)(2,1)S(1)} %shard_map.138), channel_id=1, replica_groups=mesh['x'=4,'z'=16,'c'=2,'y'=4] {'z'}, dimensions={0} | all-to-all | bytes 8192 | tf_op jit(solution)/shard_map/all_to_all | solution.py:308
  141.3 0.6 shard_map.139
Async XLA Ops:
  0.6 29.0 %copy-start.8 = (bf16[16,8]{0,1:T(8,128)(2,1)S(1)}, bf16[16,8]{0,1:T(8,128)(2,1)}, u32[]{:S(2)}) copy-start(bf16[16,8]{0,1:T(8,128)(2,1)} %param.16) | copy-start | bytes 772
  0.6 29.0 %copy-start.9 = (s32[16]{0:T(128)S(1)}, s32[16]{0:T(128)}, u32[]{:S(2)}) copy-start(s32[16]{0:T(128)} %param.15) | copy-start | bytes 196
  0.7 49.2 %copy-start.4 = (bf16[16,32,512]{2,1,0:T(8,128)(2,1)S(1)}, bf16[16,32,512]{2,1,0:T(8,128)(2,1)}, u32[]{:S(2)}) copy-start(bf16[16,32,512]{2,1,0:T(8,128)(2,1)} %values.1) | copy-start | bytes 1572868
  1.7 48.2 %copy-start.3 = (bf16[16,32,512]{2,1,0:T(8,128)(2,1)S(1)}, bf16[16,32,512]{2,1,0:T(8,128)(2,1)}, u32[]{:S(2)}) copy-start(bf16[16,32,512]{2,1,0:T(8,128)(2,1)} %keys.1) | copy-start | bytes 1572868
  49.9 63.0 %copy-start.2 = (bf16[128,4096]{1,0:T(8,128)(2,1)S(1)}, bf16[128,4096]{1,0:T(8,128)(2,1)}, u32[]{:S(2)}) copy-start(bf16[128,4096]{1,0:T(8,128)(2,1)} %w_down.1) | copy-start | bytes 3145732
  50.7 62.2 %copy-start.1 = (bf16[128,4096]{1,0:T(8,128)(2,1)S(1)}, bf16[128,4096]{1,0:T(8,128)(2,1)}, u32[]{:S(2)}) copy-start(bf16[128,4096]{1,0:T(8,128)(2,1)} %w_up.1) | copy-start | bytes 3145732
  64.2 48.6 %copy-start = (bf16[128,4096]{1,0:T(8,128)(2,1)S(1)}, bf16[128,4096]{1,0:T(8,128)(2,1)}, u32[]{:S(2)}) copy-start(bf16[128,4096]{1,0:T(8,128)(2,1)} %w_gate.1) | copy-start | bytes 3145732
  81.1 16.1 %copy-start.5 = (s32[16,8]{0,1:T(8,128)S(1)}, s32[16,8]{0,1:T(8,128)}, u32[]{:S(2)}) copy-start(s32[16,8]{0,1:T(8,128)} %param.19) | copy-start | bytes 1540
  97.5 15.3 %copy-start.6 = (bf16[4096]{0:T(1024)(128)(2,1)S(1)}, bf16[4096]{0:T(1024)(128)(2,1)}, u32[]{:S(2)}) copy-start(bf16[4096]{0:T(1024)(128)(2,1)} %param.18) | copy-start | bytes 24580
  97.5 15.3 %copy-start.7 = (f32[16,8]{0,1:T(8,128)S(1)}, f32[16,8]{0,1:T(8,128)}, u32[]{:S(2)}) copy-start(f32[16,8]{0,1:T(8,128)} %param.20) | copy-start | bytes 1540
